TPU v7x, 128 devices: a whole 4x4x4 slice. The times are simulated.
128 devices in a mesh: dom: 64 (over z_lo, x, y, core), edge: 2 (over z_hi).
Axes of the slice: x: 4, y: 4, z: 4 (z_hi: 2, z_lo: 2; z = z_hi * 2 + z_lo), core: 2. Of those that a mesh axis runs over, the one named last changes fastest.
Arguments:
- entities: bfloat16 [131072, 400], P('dom'), may hold values from -1.1953125 to 1.1953125
- relations: bfloat16 [1345, 400], replicated, may hold values from -6 to 6
- matching: int32 [64], replicated, may hold values from 0 to 63, each once
- group_counts: int32 [64, 2], P('dom'), may hold values from 1 to 6, as said below
- left_rows: int32 [64, 2, 6, 512], P('dom', None, 'edge'), may hold values from 0 to 2047
- right_rows: int32 [64, 2, 6, 512], P('dom', None, 'edge'), may hold values from 0 to 2047
- relation_ids: int32 [64, 2, 6, 512], P('dom', None, 'edge'), may hold values from 0 to 1344
- negative_rows: int32 [64, 2, 6, 1024], P('dom', None, 'edge'), may hold values from 0 to 2047
Outputs:
- entity_grad: float32 [131072, 400], P('dom')
- relation_grad: float32 [1345, 400], replicated
Inputs may be any that keep to these rules, and one draw needn't show every extreme that they name: `group_counts`: live slots come first in each bucket; some bucket has all 6 slots live in every draw.
All inputs are finite; a program needn't handle non-finite values.
Results may differ from a plain program's by a relative error of at most 0.0003.
Values may be sent and summed in bfloat16 or wider, within the bound.
No kernel may reach another device: no remote copies, remote signals or barrier semaphores. Data moves between devices by JAX's collectives and lax.ppermute only.
A program may use at most 128 MiB of HBM per device.

v0:
```python
import jax
import jax.numpy as jnp
from jax import lax
from jax.sharding import PartitionSpec as P


def complex_product(left, right):
    half = left.shape[-1] // 2
    a, b = (left[..., :half], left[..., half:])
    c, d = (right[..., :half], right[..., half:])
    return jnp.concatenate([a * c - b * d, a * d + b * c], axis=-1)


def conjugate_product(grad, right):
    half = grad.shape[-1] // 2
    a, b = (grad[..., :half], grad[..., half:])
    c, d = (right[..., :half], right[..., half:])
    return jnp.concatenate([a * c + b * d, b * c - a * d], axis=-1)


def group_terms(left_slab, right_slab, relations, left_idx, right_idx, rel_idx, neg_idx):
    heads = left_slab[left_idx].astype(jnp.float32)
    rel = relations[rel_idx].astype(jnp.float32)
    tails = right_slab[right_idx].astype(jnp.float32)
    query = complex_product(heads, rel)
    positive = jnp.sum(query * tails, axis=-1)
    query_low = query.astype(jnp.bfloat16)
    negatives = right_slab[neg_idx]
    scores = lax.dot_general(
        query_low, negatives, (((1,), (1,)), ((), ())), preferred_element_type=jnp.float32
    )
    pos_grad = -jax.nn.sigmoid(-positive)
    neg_grad = (jax.nn.sigmoid(scores) * (1.0 / negatives.shape[0])).astype(jnp.bfloat16)
    query_grad = pos_grad[:, None] * tails + jnp.dot(
        neg_grad, negatives, preferred_element_type=jnp.float32
    )
    tail_grad = pos_grad[:, None] * query
    neg_rows_grad = lax.dot_general(
        neg_grad, query_low, (((0,), (0,)), ((), ())), preferred_element_type=jnp.float32
    )
    head_grad = conjugate_product(query_grad, rel)
    rel_grad = conjugate_product(query_grad, heads)
    return (head_grad, tail_grad, neg_rows_grad, rel_grad)


def body(
    entities, relations, matching, group_counts, left_rows, right_rows, relation_ids, negative_rows
):
    parts = lax.axis_size("dom")
    side = lax.axis_index("edge")
    rows, width = entities.shape
    half_slots = left_rows.shape[2]
    pieces = entities.reshape(parts, rows // parts, width)
    held = lax.all_to_all(pieces, "dom", split_axis=0, concat_axis=0, tiled=True)
    chosen = jnp.take(held, matching, axis=0)
    partner = lax.all_to_all(chosen, "dom", split_axis=0, concat_axis=0, tiled=True).reshape(
        rows, width
    )

    def run_bucket(bucket, right_slab, carry):
        live = jnp.clip(group_counts[0, bucket] - side * half_slots, 0, half_slots)
        right_base = 0 if bucket == 0 else rows

        def step(slot, state):
            both, rel_total = state
            lidx = left_rows[0, bucket, slot]
            ridx = right_rows[0, bucket, slot]
            relx = relation_ids[0, bucket, slot]
            nidx = negative_rows[0, bucket, slot]
            head_grad, tail_grad, neg_grad, rel_grad = group_terms(
                entities, right_slab, relations, lidx, ridx, relx, nidx
            )
            targets = jnp.concatenate([lidx, ridx + right_base, nidx + right_base])
            values = jnp.concatenate([head_grad, tail_grad, neg_grad], axis=0)
            both = both.at[targets].add(values)
            rel_total = rel_total.at[relx].add(rel_grad)
            return (both, rel_total)

        return lax.fori_loop(0, live, step, carry)

    state = (jnp.zeros((2 * rows, width), jnp.float32), jnp.zeros(relations.shape, jnp.float32))
    state = run_bucket(0, entities, state)
    both, rel_total = run_bucket(1, partner, state)
    own = both[:rows]
    other = both[rows:]
    order = jnp.arange(parts, dtype=jnp.int32)
    inverse = jnp.sum(jnp.where(matching[None, :] == order[:, None], order[None, :], 0), axis=1)
    count = other.shape[0]
    grad_pieces = other.reshape(parts, count // parts, width)
    grad_held = lax.all_to_all(grad_pieces, "dom", split_axis=0, concat_axis=0, tiled=True)
    grad_chosen = jnp.take(grad_held, inverse, axis=0)
    total = own + lax.all_to_all(
        grad_chosen, "dom", split_axis=0, concat_axis=0, tiled=True
    ).reshape(count, width)
    entity_grad = lax.psum(total, "edge")
    relation_grad = lax.psum(rel_total, ("dom", "edge"))
    return (entity_grad, relation_grad)


def solution(mesh):
    placed = (
        P("dom", None),
        P(),
        P(),
        P("dom", None),
        P("dom", None, "edge", None),
        P("dom", None, "edge", None),
        P("dom", None, "edge", None),
        P("dom", None, "edge", None),
    )
    return jax.shard_map(
        body, mesh=mesh, in_specs=placed, out_specs=(P("dom", None), P()), check_vma=False
    )
```

profile of v0, /device:TPU:1, one launch (start us, length us, event | category | flops | bytes accessed | tf_op | source)
XLA Modules:
  0.0 942.8 jit_solution(16720007201117542630)
XLA Ops:
  10.9 10.5 %all-to-all-start = ((bf16[64,32,400]{2,1,0:T(8,128)(2,1)}), bf16[64,32,400]{2,1,0:T(8,128)(2,1)S(1)}, u32[]{:S(2)}, u32[]{:S(2)}) async-start(bf16[64,32,400]{2,1,0:T(8,128)(2,1)} %bitcast.22), calls=%async_computation | async-start | bytes 4194304 | tf_op jit(solution)/shard_map/all_to_all | solution.py:54
  25.3 24.6 %all-to-all-done = bf16[64,32,400]{2,1,0:T(8,128)(2,1)S(1)} async-done(((bf16[64,32,400]{2,1,0:T(8,128)(2,1)}), bf16[64,32,400]{2,1,0:T(8,128)(2,1)S(1)}, u32[]{:S(2)}, u32[]{:S(2)}) %all-to-all-start) | async-done | bytes 1638432 | tf_op jit(solution)/shard_map/all_to_all | solution.py:54
  55.0 5.4 all-to-all-start.1
  65.1 233.4 %while.24 = (s32[]{:T(128)}, f32[4096,400]{1,0:T(8,128)}, f32[1345,400]{1,0:T(8,128)S(1)}, s32[]{:T(128)}, s32[1,2,3,512]{3,2,1,0:T(4,128)S(1)}, /*index=5*/s32[...) while((s32[]{:T(128)}, f32[4096,400]{1,0:T(8,128)}, ...), condition=%wide.region_4.5_spmd, body=%wide.region_0.4_spmd.sunk | while | flops 1270356480 | bytes 78713224 | solution.py:79
  88.8 7.0 gather_fusion
  120.2 19.8 %scatter_fusion = f32[4096,400]{1,0:T(8,128)} fusion(f32[4096,400]{1,0:T(8,128)} %get-tuple-element.447, s32[2048]{0:T(1024)S(1)} %bitcast.98, f32[2048,400]{1,0:T(8,128)} %copy.85), kind=kCustom, calls=%fused_computation.10.clone.1 | custom fusion | flops 819200 | bytes 9838592 | tf_op jit(solution)/shard_map/while/body/scatter-add | solution.py:75
  163.3 7.0 gather_fusion
  194.8 19.8 %scatter_fusion = f32[4096,400]{1,0:T(8,128)} fusion(f32[4096,400]{1,0:T(8,128)} %get-tuple-element.447, s32[2048]{0:T(1024)S(1)} %bitcast.98, f32[2048,400]{1,0:T(8,128)} %copy.85), kind=kCustom, calls=%fused_computation.10.clone.1 | custom fusion | flops 819200 | bytes 9838592 | tf_op jit(solution)/shard_map/while/body/scatter-add | solution.py:75
  237.8 7.0 gather_fusion
  253.8 5.2 scatter_fusion.1
  269.3 19.8 %scatter_fusion = f32[4096,400]{1,0:T(8,128)} fusion(f32[4096,400]{1,0:T(8,128)} %get-tuple-element.447, s32[2048]{0:T(1024)S(1)} %bitcast.98, f32[2048,400]{1,0:T(8,128)} %copy.85), kind=kCustom, calls=%fused_computation.10.clone.1 | custom fusion | flops 819200 | bytes 9838592 | tf_op jit(solution)/shard_map/while/body/scatter-add | solution.py:75
  299.1 223.4 %while.25 = (s32[]{:T(128)}, f32[4096,400]{1,0:T(8,128)}, f32[1345,400]{1,0:T(8,128)S(1)}, s32[]{:T(128)}, s32[1,2,3,512]{3,2,1,0:T(4,128)S(1)}, /*index=5*/s32[...) while((s32[]{:T(128)}, f32[4096,400]{1,0:T(8,128)}, ...), condition=%wide.region_9.10_spmd, body=%wide.region_5.0_spmd.sunk | while | flops 1270358016 | bytes 78719384 | solution.py:79
  322.3 7.0 gather_fusion.4
  353.8 19.8 %scatter_fusion.2 = f32[4096,400]{1,0:T(8,128)} fusion(f32[4096,400]{1,0:T(8,128)} %get-tuple-element.487, s32[2048]{0:T(1024)S(1)} %bitcast.99, f32[2048,400]{1,0:T(8,128)} %copy.90), kind=kCustom, calls=%fused_computation.12.clone.1 | custom fusion | flops 819200 | bytes 9838592 | tf_op jit(solution)/shard_map/while/body/scatter-add | solution.py:75
  396.8 7.0 gather_fusion.4
  428.2 19.8 %scatter_fusion.2 = f32[4096,400]{1,0:T(8,128)} fusion(f32[4096,400]{1,0:T(8,128)} %get-tuple-element.487, s32[2048]{0:T(1024)S(1)} %bitcast.99, f32[2048,400]{1,0:T(8,128)} %copy.90), kind=kCustom, calls=%fused_computation.12.clone.1 | custom fusion | flops 819200 | bytes 9838592 | tf_op jit(solution)/shard_map/while/body/scatter-add | solution.py:75
  471.3 7.0 gather_fusion.4
  487.2 5.2 scatter_fusion.3
  502.7 19.8 %scatter_fusion.2 = f32[4096,400]{1,0:T(8,128)} fusion(f32[4096,400]{1,0:T(8,128)} %get-tuple-element.487, s32[2048]{0:T(1024)S(1)} %bitcast.99, f32[2048,400]{1,0:T(8,128)} %copy.90), kind=kCustom, calls=%fused_computation.12.clone.1 | custom fusion | flops 819200 | bytes 9838592 | tf_op jit(solution)/shard_map/while/body/scatter-add | solution.py:75
  527.1 9.1 all-to-all-start.2
  536.4 52.5 %all-to-all-done.2 = f32[64,32,400]{2,1,0:T(8,128)} async-done(((f32[64,32,400]{2,1,0:T(8,128)}), f32[64,32,400]{2,1,0:T(8,128)}, u32[]{:S(2)}, u32[]{:S(2)}) %all-to-all-start.2) | async-done | bytes 3276832 | tf_op jit(solution)/shard_map/all_to_all | solution.py:90
  596.3 61.6 %all_to_all.20 = f32[64,32,400]{2,1,0:T(8,128)S(1)} all-to-all(f32[64,32,400]{2,1,0:T(8,128)S(1)} %broadcast_select_fusion), channel_id=1, replica_groups=mesh['dom'=64,'edge'=2] {'dom'}, dimensions={0} | all-to-all | bytes 6553600 | tf_op jit(solution)/shard_map/all_to_all | solution.py:92
  665.3 110.6 %all-reduce.3.cloned.1.call-done = f32[2048,400]{1,0:T(8,128)} async-done(((f32[2048,400]{1,0:T(8,128)}), f32[2048,400]{1,0:T(8,128)}) %all-reduce.3.cloned.1.call-update) | async-done | bytes 3276816 | tf_op jit(solution)/shard_map/psum | solution.py:95
  781.1 151.5 %all-reduce.5.cloned.1.call-done = f32[1345,400]{0,1:T(8,128)} async-done(((f32[1345,400]{0,1:T(8,128)}), f32[1345,400]{0,1:T(8,128)}) %all-reduce.5.cloned.1.call-update) | async-done | bytes 2152016 | tf_op jit(solution)/shard_map/psum | solution.py:96
  (318 shorter events, 319.2 us)
Async XLA Ops:
  10.9 10.5 %copy-start.20 = (s32[1,2]{1,0:T(1,128)S(1)}, s32[1,2]{1,0:T(1,128)}, u32[]{:S(2)}) copy-start(s32[1,2]{1,0:T(1,128)} %param.15) | copy-start | bytes 28
  10.9 14.3 %copy-start.16 = (s32[1,2,3,1024]{3,1,2,0:T(2,128)S(1)}, s32[1,2,3,1024]{3,1,2,0:T(2,128)}, u32[]{:S(2)}) copy-start(s32[1,2,3,1024]{3,1,2,0:T(2,128)} %param.19) | copy-start | bytes 73732
  10.9 14.3 %copy-start.17 = (s32[1,2,3,512]{3,1,2,0:T(2,128)S(1)}, s32[1,2,3,512]{3,1,2,0:T(2,128)}, u32[]{:S(2)}) copy-start(s32[1,2,3,512]{3,1,2,0:T(2,128)} %param.16) | copy-start | bytes 36868
  10.9 14.3 %copy-start.18 = (s32[1,2,3,512]{3,1,2,0:T(2,128)S(1)}, s32[1,2,3,512]{3,1,2,0:T(2,128)}, u32[]{:S(2)}) copy-start(s32[1,2,3,512]{3,1,2,0:T(2,128)} %param.17) | copy-start | bytes 36868
  10.9 14.3 %copy-start.19 = (s32[1,2,3,512]{3,1,2,0:T(2,128)S(1)}, s32[1,2,3,512]{3,1,2,0:T(2,128)}, u32[]{:S(2)}) copy-start(s32[1,2,3,512]{3,1,2,0:T(2,128)} %param.18) | copy-start | bytes 36868
  10.9 14.3 %copy-start.21 = (s32[64]{0:T(128)S(1)}, s32[64]{0:T(128)}, u32[]{:S(2)}) copy-start(s32[64]{0:T(128)} %param.14) | copy-start | bytes 772
  10.9 38.9 %all-to-all-start = ((bf16[64,32,400]{2,1,0:T(8,128)(2,1)}), bf16[64,32,400]{2,1,0:T(8,128)(2,1)S(1)}, u32[]{:S(2)}, u32[]{:S(2)}) async-start(bf16[64,32,400]{2,1,0:T(8,128)(2,1)} %bitcast.22), calls=%async_computation | async-start | bytes 4194304 | tf_op jit(solution)/shard_map/all_to_all | solution.py:54
  55.0 244.1 %all-to-all-start.1 = ((bf16[64,32,400]{2,1,0:T(8,128)(2,1)}), bf16[64,32,400]{2,1,0:T(8,128)(2,1)}, u32[]{:S(2)}, u32[]{:S(2)}) async-start(bf16[64,32,400]{2,1,0:T(8,128)(2,1)} %broadcast_select_fusion.1), calls=%async_computation.1 | async-start | bytes 4194304 | tf_op jit(solution)/shard_map/all_to_all | solution.py:56
  110.0 3.2 copy-start.12
  110.0 3.2 copy-start.13
  184.5 3.2 copy-start.12
  184.5 3.2 copy-start.13
  259.0 3.2 copy-start.12
  259.0 3.2 copy-start.13
  343.5 3.2 copy-start.14
  343.5 3.2 copy-start.15
  418.0 3.2 copy-start.14
  418.0 3.2 copy-start.15
  492.4 3.2 copy-start.14
  492.4 3.2 copy-start.15
  527.1 9.2 copy-start.22
  527.1 61.8 %all-to-all-start.2 = ((f32[64,32,400]{2,1,0:T(8,128)}), f32[64,32,400]{2,1,0:T(8,128)}, u32[]{:S(2)}, u32[]{:S(2)}) async-start(f32[64,32,400]{2,1,0:T(8,128)} %bitcast.97), calls=%async_computation.2 | async-start | bytes 8388608 | tf_op jit(solution)/shard_map/all_to_all | solution.py:90
  536.2 239.7 %all-reduce.3.cloned.1.call-start = ((), (), s32[]{:S(2)}) async-start(), calls=%async_computation.4 | async-start | bytes 8388608 | tf_op jit(solution)/shard_map/psum | solution.py:95
  663.1 269.5 %all-reduce.5.cloned.1.call-start = ((), (), s32[]{:S(2)}) async-start(), calls=%async_computation.5 | async-start | bytes 4505600 | tf_op jit(solution)/shard_map/psum | solution.py:96
  (36 other events, 73.4 us)
Sparse Core Ops, SparseCore 0:
  663.2 112.6 all-reduce.2
  782.1 150.4 all-reduce.4
where the time goes:
time: 951 us; the launch traced here: 943 us
  waiting for transfers between devices  339 us (36%)
  other arithmetic  233 us (25%)
  local copies, waits for them, and re-layouts  227 us (24%)
  blocking collectives  61.6 us (6%)
  matrix products  30.6 us (3%)
  starting transfers between devices  25.1 us (3%)
  between operations  15.7 us (2%)
  loops' own time  11.1 us (1%)
    psum x1, waiting for transfers between devices, body(): relation_grad = lax.psum(rel_total, ('dom', 'edge'))  152 us
    scatter-add x6, other arithmetic, step(): both = both.at[targets].add(values)  119 us
    psum x1, waiting for transfers between devices, body(): entity_grad = lax.psum(total, 'edge')  111 us
    all_to_all x1, blocking collectives, body(): lax.all_to_all(grad_chosen, 'dom', split_axis=0, concat_axis=0, tiled=True)  61.6 us
    all_to_all x1, waiting for transfers between devices, body(): lax.all_to_all(grad_pieces, 'dom', split_axis=0, concat_axis=0, tiled=True)  52.5 us
    gather x6, local copies, waits for them, and re-layouts, group_terms(): negatives = right_slab[neg_idx]  41.9 us
    gather x12, local copies, waits for them, and re-layouts, group_terms(): tails = right_slab[right_idx].astype(jnp.float32)  39 us
    scatter-add x6, other arithmetic, step(): rel_total = rel_total.at[relx].add(rel_grad)  31.3 us
  transfers between devices with their start and end apart: 5, of which 4 were waited for; matrix products, arithmetic and copies ran while one was open for 25% of the time, Pallas kernels for 0%

commit v1 on v0

v1 whole, which is shorter than its diff:
```python
import jax
import jax.numpy as jnp
from jax import lax
from jax.experimental import pallas as pl
from jax.experimental.pallas import tpu as pltpu
from jax.sharding import PartitionSpec as P

F32 = jnp.float32
BF16 = jnp.bfloat16
CHUNK = 512
VM = pl.BlockSpec(memory_space=pltpu.VMEM)
SM = pl.BlockSpec(memory_space=pltpu.SMEM)
PARAMS = pltpu.CompilerParams(vmem_limit_bytes=58 * 2**20)

LANES = 128
SLAB_WINDOW = 112
SLAB_STARTS = (0, 96, 192, 288)
GRAD_WINDOW = 56
GRAD_STARTS = (0, 56, 112, 168, 224, 280, 336, 344)


def nn(a, b):
    return lax.dot_general(a, b, (((1,), (0,)), ((), ())), preferred_element_type=F32)


def nt(a, b):
    return lax.dot_general(a, b, (((1,), (1,)), ((), ())), preferred_element_type=F32)


def one_hot(idx, first, count):
    rows = lax.broadcasted_iota(jnp.int32, (count, idx.shape[1]), 0) + first
    return (rows == idx).astype(F32).astype(BF16)


def row_counts(idx, rows):
    high = one_hot(idx >> 7, 0, rows // LANES)
    low = one_hot(idx & (LANES - 1), 0, LANES)
    table = nt(high, low)
    return jnp.concatenate([table[i : i + 1, :] for i in range(rows // LANES)], axis=1)


def split(x):
    high = x.astype(BF16)
    return high, (x - high.astype(F32)).astype(BF16)


def sigmoid(x):
    return 1.0 / (1.0 + jnp.exp(-x))


def group(slot, left, right, by_row, relations, idx, marks, rel_marks, neg, own, other, rel_total):
    lidx, ridx, relx, nidx = [ref[slot] for ref in idx]
    edges, negatives = lidx.shape[1], nidx.shape[1]
    width, rows = left.shape
    half = width // 2
    parts = [slice(c, c + CHUNK) for c in range(0, rows, CHUNK)]
    for s in parts:
        marks[s, :edges] = one_hot(lidx, s.start, CHUNK)
        marks[s, edges:] = one_hot(ridx, s.start, CHUNK)
    rel_marks[...] = one_hot(relx, 0, relations.shape[1])
    h = nn(left[...], marks[:, :edges])
    t = nn(right[...], marks[:, edges:])
    rel = nn(relations[...], rel_marks[...])
    ha, hb, ra, rb = h[:half], h[half:], rel[:half], rel[half:]
    query = jnp.concatenate([ha * ra - hb * rb, ha * rb + hb * ra], axis=0)
    positive = jnp.sum(query * t, axis=0, keepdims=True)
    pos_grad = -sigmoid(-positive)
    query_low = query.astype(BF16)
    counts = row_counts(nidx, rows)
    for s in parts:
        scores = nn(by_row[s, :], query_low)
        neg[s, :] = (sigmoid(scores) * (1.0 / negatives)).astype(BF16)
    counted_high, counted_low = split(right[...].astype(F32) * counts)
    query_grad = pos_grad * t + nn(counted_high, neg[...]) + nn(counted_low, neg[...])
    ga, gb = query_grad[:half], query_grad[half:]
    head_high, head_low = split(jnp.concatenate([ga * ra + gb * rb, gb * ra - ga * rb], axis=0))
    rel_high, rel_low = split(jnp.concatenate([ga * ha + gb * hb, gb * ha - ga * hb], axis=0))
    tail_high, tail_low = split(pos_grad * query)
    for s in parts:
        neg_rows = nt(query_low, neg[s, :]) * counts[:, s]
        if other is None:
            both_high = jnp.concatenate([head_high, tail_high], axis=1)
            both_low = jnp.concatenate([head_low, tail_low], axis=1)
            own[:, s] += nt(both_high, marks[s, :]) + nt(both_low, marks[s, :]) + neg_rows
        else:
            own[:, s] += nt(head_high, marks[s, :edges]) + nt(head_low, marks[s, :edges])
            other[:, s] += (
                nt(tail_high, marks[s, edges:]) + nt(tail_low, marks[s, edges:]) + neg_rows
            )
    rel_total[...] += nt(rel_high, rel_marks[...]) + nt(rel_low, rel_marks[...])


def first_kernel(span, left, relations, lidx, ridx, relx, nidx, own, rel_total, by_row, marks, rel_marks, neg):
    own[...] = jnp.zeros_like(own)
    rel_total[...] = jnp.zeros_like(rel_total)
    by_row[...] = left[...].T

    def step(slot, _):
        group(slot, left, left, by_row, relations, (lidx, ridx, relx, nidx), marks, rel_marks, neg, own, None, rel_total)
        return 0

    lax.fori_loop(span[0], span[1], step, 0)


def more_kernel(span, left, relations, lidx, ridx, relx, nidx, own_in, rel_in, own, rel_total, by_row, marks, rel_marks, neg):
    own[...] = own_in[...]
    rel_total[...] = rel_in[...]
    by_row[...] = left[...].T

    def step(slot, _):
        group(slot, left, left, by_row, relations, (lidx, ridx, relx, nidx), marks, rel_marks, neg, own, None, rel_total)
        return 0

    lax.fori_loop(span[0], span[1], step, 0)


def second_kernel(
    span, left, pieces, relations, lidx, ridx, relx, nidx, own_in, rel_in,
    keep, give, other_pieces, rel_out, right, own, other, rel_total, by_row, marks, rel_marks, neg,
):
    own[...] = own_in[...]
    rel_total[...] = rel_in[...]
    other[...] = jnp.zeros_like(other)
    count = len(SLAB_STARTS)
    for j in range(pieces.shape[0]):
        lane, start = (j // count) * LANES, SLAB_STARTS[j % count]
        right[start : start + SLAB_WINDOW, lane : lane + LANES] = pieces[j]
    by_row[...] = right[...].T

    def step(slot, _):
        group(slot, left, right, by_row, relations, (lidx, ridx, relx, nidx), marks, rel_marks, neg, own, other, rel_total)
        return 0

    lax.fori_loop(0, span[1], step, 0)
    rel_out[...] = rel_total[:, : rel_out.shape[1]]
    side = span[2]
    middle = own.shape[1] // 2

    @pl.when(side == 0)
    def _():
        keep[...] = own[:, :middle]
        give[...] = own[:, middle:]

    @pl.when(side != 0)
    def _():
        keep[...] = own[:, middle:]
        give[...] = own[:, :middle]

    count = len(GRAD_STARTS)
    for j in range(other_pieces.shape[0] // 2):
        lane, start = (j // count) * LANES, GRAD_STARTS[j % count]
        for s in range(2):
            first = lane + s * middle
            other_pieces[2 * j + s] = other[start : start + GRAD_WINDOW, first : first + LANES]


def cut_kernel(slab, pieces):
    count = len(SLAB_STARTS)
    for j in range(pieces.shape[0]):
        lane, start = (j // count) * LANES, SLAB_STARTS[j % count]
        pieces[j] = slab[start : start + SLAB_WINDOW, lane : lane + LANES]


def take_kernel(matching, held, chosen):
    def step(q, _):
        chosen[q] = held[matching[q]]
        return 0

    lax.fori_loop(0, chosen.shape[0], step, 0)


def merge_kernel(matching, held, chosen):
    def step(q, _):
        chosen[matching[q]] = held[2 * q] + held[2 * q + 1]
        return 0

    lax.fori_loop(0, chosen.shape[0], step, 0)


def add_kernel(keep, got, pieces, out):
    count = len(GRAD_STARTS)
    for j in range(pieces.shape[0]):
        at = (slice(GRAD_STARTS[j % count], GRAD_STARTS[j % count] + GRAD_WINDOW), slice((j // count) * LANES, (j // count + 1) * LANES))
        out[at] = keep[at] + got[at] + pieces[j]


def join_kernel(side, mine, theirs, out):
    middle = mine.shape[1]

    @pl.when(side[0] == 0)
    def _():
        out[:, :middle] = mine[...]
        out[:, middle:] = theirs[...]

    @pl.when(side[0] != 0)
    def _():
        out[:, :middle] = theirs[...]
        out[:, middle:] = mine[...]


def call(kernel, outs, specs, scratch, *args, flops=0, moved=0):
    return pl.pallas_call(
        kernel,
        out_shape=outs,
        in_specs=specs,
        out_specs=jax.tree.map(lambda _: VM, outs),
        scratch_shapes=scratch,
        compiler_params=PARAMS,
        cost_estimate=pl.CostEstimate(flops=flops, bytes_accessed=moved, transcendentals=0),
    )(*args)


def body(entities, relations, matching, group_counts, left_rows, right_rows, relation_ids, negative_rows):
    parts = lax.axis_size("dom")
    side = lax.axis_index("edge")
    rows, width = entities.shape
    half_slots, edges = left_rows.shape[2:]
    rels = relations.shape[0]
    padded = -(-rels // LANES) * LANES
    middle = rows // 2

    slab = entities.T
    pieces = call(cut_kernel, jax.ShapeDtypeStruct((parts, SLAB_WINDOW, LANES), BF16), [VM], [], slab)
    held = lax.all_to_all(pieces, "dom", split_axis=0, concat_axis=0, tiled=True)

    rel_wide = jnp.pad(relations.T, ((0, 0), (0, padded - rels)))
    live = jnp.clip(group_counts[0] - side * half_slots, 0, half_slots).astype(jnp.int32)
    idx = [
        [ref[0, b].reshape(half_slots, 1, ref.shape[3]) for ref in (left_rows, right_rows, relation_ids, negative_rows)]
        for b in range(2)
    ]
    work = [
        pltpu.VMEM((rows, width), BF16),
        pltpu.VMEM((rows, 2 * edges), BF16),
        pltpu.VMEM((padded, edges), BF16),
        pltpu.VMEM((rows, edges), BF16),
    ]
    sums = (jax.ShapeDtypeStruct((width, rows), F32), jax.ShapeDtypeStruct((width, padded), F32))
    unit = 2 * width * rows * edges * 12
    zero = jnp.zeros((), jnp.int32)
    span_a = jnp.stack([zero, jnp.minimum(live[0], 1)])
    span_b = jnp.stack([zero + 1, live[0]])
    own, rel_total = call(first_kernel, sums, [SM] + [VM] * 6, work, span_a, slab, rel_wide, *idx[0], flops=unit)
    chosen = call(take_kernel, jax.ShapeDtypeStruct(held.shape, BF16), [SM, VM], [], matching, held)
    partner = lax.all_to_all(chosen, "dom", split_axis=0, concat_axis=0, tiled=True)
    own, rel_total = call(
        more_kernel, sums, [SM] + [VM] * 8, work, span_b, slab, rel_wide, *idx[0], own, rel_total, flops=2 * unit
    )
    span_c = jnp.stack([zero, live[1], side.astype(jnp.int32)])
    halves = jax.ShapeDtypeStruct((width, middle), F32)
    keep, give, other, rel_part = call(
        second_kernel,
        (
            halves,
            halves,
            jax.ShapeDtypeStruct((2 * parts, GRAD_WINDOW, LANES), F32),
            jax.ShapeDtypeStruct((width, rels), F32),
        ),
        [SM] + [VM] * 9,
        [
            pltpu.VMEM((width, rows), BF16),
            pltpu.VMEM((width, rows), F32),
            pltpu.VMEM((width, rows), F32),
            pltpu.VMEM((width, padded), F32),
        ]
        + work,
        span_c, slab, partner, rel_wide, *idx[1], own, rel_total,
        flops=3 * unit,
    )
    swap = [(0, 1), (1, 0)]
    relation_grad = lax.psum(rel_part, ("dom", "edge"))
    got = lax.ppermute(give, "edge", swap)
    grad_held = lax.all_to_all(other, ("dom", "edge"), split_axis=0, concat_axis=0, tiled=True)
    merged = call(
        merge_kernel, jax.ShapeDtypeStruct((parts, GRAD_WINDOW, LANES), F32), [SM, VM], [], matching, grad_held
    )
    grad_pieces = lax.all_to_all(merged, "dom", split_axis=0, concat_axis=0, tiled=True)
    mine = call(add_kernel, halves, [VM] * 3, [], keep, got, grad_pieces)
    theirs = lax.ppermute(mine, "edge", swap)
    total = call(
        join_kernel, jax.ShapeDtypeStruct((width, rows), F32), [SM, VM, VM], [], side.astype(jnp.int32)[None], mine, theirs
    )
    return total.T, relation_grad.T


def solution(mesh):
    placed = (
        P("dom", None),
        P(),
        P(),
        P("dom", None),
        P("dom", None, "edge", None),
        P("dom", None, "edge", None),
        P("dom", None, "edge", None),
        P("dom", None, "edge", None),
    )
    return jax.shard_map(
        body, mesh=mesh, in_specs=placed, out_specs=(P("dom", None), P()), check_vma=False
    )
```

time: 951 us -> 442 us (0.46)
  other arithmetic: 233 us -> 3.04 us
  local copies, waits for them, and re-layouts: 227 us -> 12.2 us
  waiting for transfers between devices: 339 us -> 224 us
  Pallas kernels: 0 us -> 85.4 us
  matrix products: 30.6 us -> 0 us
  loops' own time: 11.1 us -> 0 us
  blocking collectives: 61.6 us -> 71.4 us
    scatter-add x12 -> x0, other arithmetic: 150 us -> none  [the longest x6 119 us: step(): both = both.at[targets].add(values)]
    gather x44 -> x0, local copies, waits for them, and re-layouts: 143 us -> none  [the longest x6 41.9 us: group_terms(): negatives = right_slab[neg_idx]]
    psum x2 -> x1, waiting for transfers between devices: 262 us -> 120 us  [body(): relation_grad = lax.psum(rel_part, ('dom', 'edge'))]
    ppermute x0 -> x2, waiting for transfers between devices: none -> 94.9 us  [the longest x1 55.8 us: body(): got = lax.ppermute(give, 'edge', swap)]
    pallas_call x0 -> x8, Pallas kernels: none -> 85.4 us  [call(): pl.pallas_call(kernel, out_shape=outs, in_specs=specs, out_specs=jax.tree...]
    all_to_all x1, waiting for transfers between devices: 52.5 us -> 0.01 us  [body(): lax.all_to_all(merged, 'dom', split_axis=0, concat_axis=0, tiled=True)]
    concatenate x12 -> x0, local copies, waits for them, and re-layouts: 45.2 us -> none  [the longest x6 30.1 us: step(): values = jnp.concatenate([head_grad, tail_grad, neg_grad], axis=0)]
    dot_general x18 -> x0, matrix products: 30.6 us -> none  [the longest x6 15.1 us: group_terms(): lax.dot_general(query_low, negatives, (((1,), (1,)), ((), ())), preferred...]
  transfers between devices with their start and end apart: 5 -> 6, of which waited for: 4 -> 5; matrix products, arithmetic and copies ran while one was open for 25% -> 2% of each run, Pallas kernels for 0% -> 9%
where the time goes in v1:
time: 442 us; the launch traced here: 438 us
  waiting for transfers between devices  224 us (51%)
  Pallas kernels  85.4 us (19%)
  blocking collectives  71.4 us (16%)
  starting transfers between devices  27.2 us (6%)
  between operations  15 us (3%)
  local copies, waits for them, and re-layouts  12.2 us (3%)
    psum x1, waiting for transfers between devices, body(): relation_grad = lax.psum(rel_part, ('dom', 'edge'))  120 us
    pallas_call x8, Pallas kernels, call(): pl.pallas_call(kernel, out_shape=outs, in_specs=specs, out_specs=jax.tree...  85.4 us
    all_to_all x1, blocking collectives, body(): lax.all_to_all(other, ('dom', 'edge'), split_axis=0, concat_axis=0, tiled...  71.4 us
    ppermute x1, waiting for transfers between devices, body(): got = lax.ppermute(give, 'edge', swap)  55.8 us
    ppermute x1, waiting for transfers between devices, body(): theirs = lax.ppermute(mine, 'edge', swap)  39.2 us
    all_to_all x1, starting transfers between devices, body(): lax.all_to_all(pieces, 'dom', split_axis=0, concat_axis=0, tiled=True)  10.5 us
  transfers between devices with their start and end apart: 6, of which 5 were waited for; matrix products, arithmetic and copies ran while one was open for 2% of the time, Pallas kernels for 9%

profile of v1, /device:TPU:1, one launch (start us, length us, event | category | flops | bytes accessed | tf_op | source)
XLA Modules:
  0.0 438.4 jit_solution(463678713099202250)
XLA Ops:
  7.2 3.0 shard_map.95
  10.2 10.5 %all-to-all-start = ((bf16[64,112,128]{2,1,0:T(8,128)(2,1)}), bf16[64,112,128]{2,1,0:T(8,128)(2,1)S(1)}, u32[]{:S(2)}, u32[]{:S(2)}) async-start(bf16[64,112,128]{2,1,0:T(8,128)(2,1)} %shard_map.95), calls=%async_computation | async-start | bytes 3670016 | tf_op jit(solution)/shard_map/all_to_all | solution.py:224
  22.0 1.3 pad_add_fusion.1.span
  28.0 16.6 %shard_map.97 = (f32[400,2048]{1,0:T(8,128)}, f32[400,1408]{1,0:T(8,128)}) custom-call(s32[2]{0:T(128)} %pad_add_fusion.2.span, bf16[400,2048]{1,0:T(8,128)(2,1)} %bitcast.42, bf16[400,1408]{1,0:T(8,128)(2,1)} %pad.4.relations, s32[3,1,512]{2,1,0:T(1,128)} %get-tuple-element.24.lidx, s32[3,1,512]{2,1,0:T(1,128)} %get-tuple-element.29.ridx, ...), custom_call_target="tpu_custom_call" | custom-call | flops 10066329600 | tf_op jit(solution)/shard_map/pallas_call | solution.py:202
  44.6 1.6 all-to-all-done.held
  46.2 1.2 copy-done
  47.4 3.2 shard_map.96
  50.7 7.3 %all-to-all-start.1 = ((bf16[64,112,128]{2,1,0:T(8,128)(2,1)}), bf16[64,112,128]{2,1,0:T(8,128)(2,1)S(1)}, u32[]{:S(2)}, u32[]{:S(2)}) async-start(bf16[64,112,128]{2,1,0:T(8,128)(2,1)} %shard_map.96), calls=%async_computation.1 | async-start | bytes 3670016 | tf_op jit(solution)/shard_map/all_to_all | solution.py:245
  58.0 18.3 %shard_map.98 = (f32[400,2048]{1,0:T(8,128)}, f32[400,1408]{1,0:T(8,128)}) custom-call(s32[2]{0:T(128)} %pad_add_fusion.1.span, bf16[400,2048]{1,0:T(8,128)(2,1)} %bitcast.43, bf16[400,1408]{1,0:T(8,128)(2,1)} %pad.4.relations, s32[3,1,512]{2,1,0:T(1,128)} %get-tuple-element.24.lidx, s32[3,1,512]{2,1,0:T(1,128)} %get-tuple-element.29.ridx, ...), custom_call_target="tpu_custom_call" | custom-call | flops 20132659200 | tf_op jit(solution)/shard_map/pallas_call | solution.py:202
  76.3 7.3 %all-to-all-done.1.pieces = bf16[64,112,128]{2,1,0:T(8,128)(2,1)S(1)} async-done(((bf16[64,112,128]{2,1,0:T(8,128)(2,1)}), bf16[64,112,128]{2,1,0:T(8,128)(2,1)S(1)}, u32[]{:S(2)}, u32[]{:S(2)}) %all-to-all-start.1) | async-done | bytes 1835040 | tf_op jit(solution)/shard_map/all_to_all | solution.py:245
  83.6 1.2 copy-done.2
  84.8 32.4 %shard_map.99 = (f32[400,1024]{1,0:T(8,128)}, f32[400,1024]{1,0:T(8,128)}, f32[128,56,128]{2,1,0:T(8,128)}, f32[400,1345]{1,0:T(8,128)}) custom-call(s32[3]{0:T(128)} %pad_add_fusion.span, bf16[400,2048]{1,0:T(8,128)(2,1)} %bitcast.44, bf16[64,112,128]{2,1,0:T(8,128)(2,1)} %copy-done.2, bf16[400,1408]{1,0:T(8,128)(2,1)} %pad.4.relations, ...), custom_call_target="tpu_custom_call" | custom-call | flops 30198988800 | tf_op jit(solution)/shard_map/pallas_call | solution.py:202
  117.2 71.4 %all_to_all.20.held = f32[128,56,128]{2,1,0:T(8,128)} all-to-all(f32[128,56,128]{2,1,0:T(8,128)} %get-tuple-element.16), channel_id=1, replica_groups=mesh['dom'=64,'edge'=2] {'dom','edge'}, dimensions={0} | all-to-all | bytes 7340032 | tf_op jit(solution)/shard_map/all_to_all | solution.py:273
  188.5 3.8 shard_map.100
  192.3 5.9 %all-to-all-start.3 = ((f32[64,56,128]{2,1,0:T(8,128)}), f32[64,56,128]{2,1,0:T(8,128)S(1)}, u32[]{:S(2)}, u32[]{:S(2)}) async-start(f32[64,56,128]{2,1,0:T(8,128)} %shard_map.100), calls=%async_computation.3 | async-start | bytes 3670016 | tf_op jit(solution)/shard_map/all_to_all | solution.py:277
  198.3 1.7 collective-permute-start
  200.0 55.8 %collective-permute-done.got = f32[400,1024]{1,0:T(8,128)S(1)} collective-permute-done((f32[400,1024]{1,0:T(8,128)}, f32[400,1024]{1,0:T(8,128)S(1)}, u32[]{:S(2)}, u32[]{:S(2)}) %collective-permute-start) | collective-permute-done | bytes 1638432 | tf_op jit(solution)/shard_map/ppermute | solution.py:272
  255.7 1.2 copy-done.3
  257.5 4.2 shard_map.101.mine
  261.6 1.9 collective-permute-start.1
  263.5 39.2 %collective-permute-done.1.theirs = f32[400,1024]{1,0:T(8,128)S(1)} collective-permute-done((f32[400,1024]{1,0:T(8,128)}, f32[400,1024]{1,0:T(8,128)S(1)}, u32[]{:S(2)}, u32[]{:S(2)}) %collective-permute-start.1) | collective-permute-done | bytes 1638432 | tf_op jit(solution)/shard_map/ppermute | solution.py:279
  303.9 3.9 shard_map.102
  307.8 120.5 %all-reduce.3.cloned.1.call-done = f32[1345,400]{0,1:T(8,128)} async-done(((f32[1345,400]{0,1:T(8,128)}), f32[1345,400]{0,1:T(8,128)}) %all-reduce.3.cloned.1.call-update) | async-done | bytes 2152016 | tf_op jit(solution)/shard_map/psum | solution.py:271
  428.2 3.1 copy.27
  (30 shorter events, 7.2 us)
Async XLA Ops:
  10.2 10.5 %copy-start.10 = (s32[1,2]{1,0:T(1,128)S(1)}, s32[1,2]{1,0:T(1,128)}, u32[]{:S(2)}) copy-start(s32[1,2]{1,0:T(1,128)} %param.11) | copy-start | bytes 28
  10.2 13.1 %copy-start.5 = (bf16[1345,400]{0,1:T(8,128)(2,1)S(1)}, bf16[1345,400]{0,1:T(8,128)(2,1)}, u32[]{:S(2)}) copy-start(bf16[1345,400]{0,1:T(8,128)(2,1)} %param.9) | copy-start | bytes 3228004
  10.2 36.1 %all-to-all-start = ((bf16[64,112,128]{2,1,0:T(8,128)(2,1)}), bf16[64,112,128]{2,1,0:T(8,128)(2,1)S(1)}, u32[]{:S(2)}, u32[]{:S(2)}) async-start(bf16[64,112,128]{2,1,0:T(8,128)(2,1)} %shard_map.95), calls=%async_computation | async-start | bytes 3670016 | tf_op jit(solution)/shard_map/all_to_all | solution.py:224
  20.6 5.5 %copy-start.7 = (s32[1,2,3,512]{3,1,2,0:T(2,128)S(1)}, s32[1,2,3,512]{3,1,2,0:T(2,128)}, u32[]{:S(2)}) copy-start(s32[1,2,3,512]{3,1,2,0:T(2,128)} %param.12) | copy-start | bytes 36868
  20.7 6.1 %copy-start.6 = (s32[1,2,3,1024]{3,1,2,0:T(2,128)S(1)}, s32[1,2,3,1024]{3,1,2,0:T(2,128)}, u32[]{:S(2)}) copy-start(s32[1,2,3,1024]{3,1,2,0:T(2,128)} %param.15) | copy-start | bytes 73732
  20.7 6.7 %copy-start.8 = (s32[1,2,3,512]{3,1,2,0:T(2,128)S(1)}, s32[1,2,3,512]{3,1,2,0:T(2,128)}, u32[]{:S(2)}) copy-start(s32[1,2,3,512]{3,1,2,0:T(2,128)} %param.14) | copy-start | bytes 36868
  20.7 6.7 %copy-start.9 = (s32[1,2,3,512]{3,1,2,0:T(2,128)S(1)}, s32[1,2,3,512]{3,1,2,0:T(2,128)}, u32[]{:S(2)}) copy-start(s32[1,2,3,512]{3,1,2,0:T(2,128)} %param.13) | copy-start | bytes 36868
  46.2 1.2 copy-start
  50.7 32.9 %all-to-all-start.1 = ((bf16[64,112,128]{2,1,0:T(8,128)(2,1)}), bf16[64,112,128]{2,1,0:T(8,128)(2,1)S(1)}, u32[]{:S(2)}, u32[]{:S(2)}) async-start(bf16[64,112,128]{2,1,0:T(8,128)(2,1)} %shard_map.96), calls=%async_computation.1 | async-start | bytes 3670016 | tf_op jit(solution)/shard_map/all_to_all | solution.py:245
  83.6 1.2 copy-start.2
  192.3 63.4 %all-to-all-start.3 = ((f32[64,56,128]{2,1,0:T(8,128)}), f32[64,56,128]{2,1,0:T(8,128)S(1)}, u32[]{:S(2)}, u32[]{:S(2)}) async-start(f32[64,56,128]{2,1,0:T(8,128)} %shard_map.100), calls=%async_computation.3 | async-start | bytes 3670016 | tf_op jit(solution)/shard_map/all_to_all | solution.py:277
  198.2 230.0 %all-reduce.3.cloned.1.call-start = ((), (), s32[]{:S(2)}) async-start(), calls=%async_computation.4 | async-start | bytes 4505600 | tf_op jit(solution)/shard_map/psum | solution.py:271
  198.3 57.5 %collective-permute-start = (f32[400,1024]{1,0:T(8,128)}, f32[400,1024]{1,0:T(8,128)S(1)}, u32[]{:S(2)}, u32[]{:S(2)}) collective-permute-start(f32[400,1024]{1,0:T(8,128)} %get-tuple-element.15), channel_id=1, source_target_pairs={{0,1},{1,0},{2,3},{3,2},{4,5},{5,4},{6,7},{7,6},{8,9},{9,8},{10,11... | collective-permute-start | bytes 4915208 | tf_op jit(solution)/shard_map/ppermute | solution.py:272
  255.7 1.2 copy-start.3
  255.7 1.8 copy-start.1
  261.6 41.1 %collective-permute-start.1 = (f32[400,1024]{1,0:T(8,128)}, f32[400,1024]{1,0:T(8,128)S(1)}, u32[]{:S(2)}, u32[]{:S(2)}) collective-permute-start(f32[400,1024]{1,0:T(8,128)} %shard_map.101.mine), channel_id=1, source_target_pairs={{0,1},{1,0},{2,3},{3,2},{4,5},{5,4},{6,7},{7,6},{8,9},{9,8},{10,11... | collective-permute-start | bytes 4915208 | tf_op jit(solution)/shard_map/ppermute | solution.py:279
  302.7 1.2 copy-start.4
Sparse Core Ops, SparseCore 0:
  263.7 164.5 all-reduce.2

commit v2 on v1

v2 whole, which is shorter than its diff:
```python
import jax
import jax.numpy as jnp
from jax import lax
from jax.experimental import pallas as pl
from jax.experimental.pallas import tpu as pltpu
from jax.sharding import PartitionSpec as P

F32 = jnp.float32
BF16 = jnp.bfloat16
CHUNK = 512
VM = pl.BlockSpec(memory_space=pltpu.VMEM)
SM = pl.BlockSpec(memory_space=pltpu.SMEM)
HB = pl.BlockSpec(memory_space=pl.ANY)
PARAMS = pltpu.CompilerParams(vmem_limit_bytes=58 * 2**20)

LANES = 128
SLAB_WINDOW = 112
SLAB_STARTS = (0, 96, 192, 288)
GRAD_WINDOW = 56
GRAD_STARTS = (0, 56, 112, 168, 224, 280, 336, 344)
REL_WINDOW = 144
REL_RING = 16


def nn(a, b):
    return lax.dot_general(a, b, (((1,), (0,)), ((), ())), preferred_element_type=F32)


def nt(a, b):
    return lax.dot_general(a, b, (((1,), (1,)), ((), ())), preferred_element_type=F32)


def tn(a, b):
    return lax.dot_general(a, b, (((0,), (0,)), ((), ())), preferred_element_type=F32)


def one_hot(idx, first, count):
    rows = lax.broadcasted_iota(jnp.int16, (count, idx.shape[1]), 0) + jnp.int16(first)
    return jnp.where(rows == idx.astype(jnp.int16), jnp.ones((), BF16), jnp.zeros((), BF16))


def mark(idx, out, lanes):
    for c in range(0, out.shape[0], LANES):
        out[c : c + LANES, lanes] = one_hot(idx, c, LANES)


def row_counts(idx, rows):
    high = one_hot(idx >> 7, 0, rows // LANES)
    low = one_hot(idx & (LANES - 1), 0, LANES)
    table = nt(high, low)
    return jnp.concatenate([table[i : i + 1, :] for i in range(rows // LANES)], axis=1)


def split(x):
    high = x.astype(BF16)
    return high, (x - high.astype(F32)).astype(BF16)


def sigmoid(x):
    return 1.0 / (1.0 + jnp.exp(-x))


def product(h, r):
    half = h.shape[0] // 2
    a, b, c, d = h[:half], h[half:], r[:half], r[half:]
    return jnp.concatenate([a * c - b * d, a * d + b * c], axis=0)


def conjugate(grad, r):
    half = grad.shape[0] // 2
    a, b, c, d = grad[:half], grad[half:], r[:half], r[half:]
    return jnp.concatenate([a * c + b * d, b * c - a * d], axis=0)


def columns(position, mine, bucket, idx):
    ours, theirs = idx
    slots = ours.shape[0]
    near = ours[jnp.minimum(position, slots - 1)]
    if theirs is None:
        row = near
    else:
        row = jnp.where(position < mine, near, theirs[jnp.clip(position - mine, 0, slots - 1)])
    row = row[bucket : bucket + 1]
    edges = row.shape[1] // 5
    return row[:, :edges], row[:, edges : 2 * edges], row[:, 2 * edges : 3 * edges], row[:, 3 * edges :]


def halves(off, rows):
    for c in range(0, rows // 2, CHUNK):
        yield slice(c, c + CHUNK), pl.ds(pl.multiple_of(off + c, CHUNK), CHUNK)


def negative_terms(query_low, slab, neg, negatives):
    for c in range(0, slab.shape[1], CHUNK):
        scores = tn(slab[:, c : c + CHUNK], query_low)
        neg[c : c + CHUNK, :] = (sigmoid(scores) * (1.0 / negatives)).astype(BF16)


def query_gradient(pos_grad, t, right, counts, neg):
    high, low = split(right[...].astype(F32) * counts)
    return pos_grad * t + nn(high, neg) + nn(low, neg)


def add_relations(grad, rel_marks, rel_total):
    high, low = split(grad)
    rel_total[...] += nt(high, rel_marks[...]) + nt(low, rel_marks[...])


def own_slot(position, slab, relations, idx, own, rel_total, marks, rel_marks, neg):
    lidx, ridx, relx, nidx = columns(position, 0, 0, (idx, None))
    edges, negatives = lidx.shape[1], nidx.shape[1]
    rows = slab.shape[1]
    left_lanes, right_lanes = slice(0, edges), slice(edges, 2 * edges)
    mark(lidx, marks, left_lanes)
    mark(ridx, marks, right_lanes)
    mark(relx, rel_marks, slice(0, edges))
    h = nn(slab[...], marks[:, left_lanes])
    t = nn(slab[...], marks[:, right_lanes])
    rel = nn(relations[...], rel_marks[...])
    query = product(h, rel)
    pos_grad = -sigmoid(-jnp.sum(query * t, axis=0, keepdims=True))
    query_low = query.astype(BF16)
    counts = row_counts(nidx, rows)
    negative_terms(query_low, slab, neg, negatives)
    query_grad = query_gradient(pos_grad, t, slab, counts, neg[...])
    head_high, head_low = split(conjugate(query_grad, rel))
    tail_high, tail_low = split(pos_grad * query)
    both_high = jnp.concatenate([head_high, tail_high], axis=1)
    both_low = jnp.concatenate([head_low, tail_low], axis=1)
    for c in range(0, rows, CHUNK):
        at = slice(c, c + CHUNK)
        own[:, at] += (
            nt(both_high, marks[at, :]) + nt(both_low, marks[at, :]) + nt(query_low, neg[at, :]) * counts[:, at]
        )
    add_relations(conjugate(query_grad, h), rel_marks, rel_total)


def widen(relations, rel_wide):
    rels = relations.shape[1]
    rel_wide[:, rels // LANES * LANES :] = jnp.zeros((rel_wide.shape[0], LANES), BF16)
    rel_wide[:, :rels] = relations[...]


def repeat(first, last, step):
    def run(i, _):
        step(i)
        return 0

    lax.fori_loop(first, last, run, 0)


def place(counts, slots):
    side = lax.axis_index("edge").astype(jnp.int32)
    core = (lax.axis_index("dom") % 2).astype(jnp.int32)
    every = [jnp.clip(counts[0, b], 0, 2 * slots) for b in range(2)]
    near = [jnp.clip(c - side * slots, 0, slots) for c in every]
    return side, core, near, every


def streams(refs, bufs, sems, i, out=False):
    k = lax.rem(i, 2)
    ends = [(b.at[k], r.at[i]) if out else (r.at[i], b.at[k]) for r, b in zip(refs, bufs)]
    return [pltpu.make_async_copy(a, b, sems.at[n, k]) for n, (a, b) in enumerate(ends)]


def begin(copies):
    for copy in copies:
        copy.start()


def finish(copies):
    for copy in copies:
        copy.wait()


def gather_kernel(counts, slab, relations, idx, theirs, heads, rels, weights, marks, rel_marks, rel_wide):
    _, _, near, every = place(counts, idx.shape[0])
    widen(relations, rel_wide)

    def step(i):
        lidx, _, relx, nidx = columns(i, near[1], 1, (idx, theirs))
        weights[i] = row_counts(nidx, slab.shape[1])
        mark(lidx, marks, slice(0, lidx.shape[1]))
        mark(relx, rel_marks, slice(0, relx.shape[1]))
        heads[i] = nn(slab[...], marks[...]).astype(BF16)
        rels[i] = nn(rel_wide[...], rel_marks[...]).astype(BF16)

    repeat(0, every[1], step)


def own_kernel(counts, slab, relations, idx, keep, give, rel_total, own, marks, rel_marks, neg, rel_wide):
    side, _, near, _ = place(counts, idx.shape[0])
    own[...] = jnp.zeros_like(own)
    rel_total[...] = jnp.zeros_like(rel_total)
    widen(relations, rel_wide)
    repeat(0, near[0], lambda i: own_slot(i, slab, rel_wide, idx, own, rel_total, marks, rel_marks, neg))
    middle = keep.shape[1]

    @pl.when(side == 0)
    def _():
        keep[...] = own[:, :middle]
        give[...] = own[:, middle:]

    @pl.when(side != 0)
    def _():
        keep[...] = own[:, middle:]
        give[...] = own[:, :middle]


def right_kernel(
    counts, pieces, idx, theirs, weights, heads, rels,
    other_pieces, pos_grads, right, tails, negs, other, marks, head, rel, tail, neg, in_sems, out_sems,
):
    side, _, near, every = place(counts, idx.shape[0])
    mine, total = near[1], every[1]

    def fetch(i):
        return streams((heads, rels), (head, rel), in_sems, i)

    def away(i):
        return streams((tails, negs), (tail, neg), out_sems, i, out=True)

    @pl.when(total >= 1)
    def _():
        begin(fetch(0))

    other[...] = jnp.zeros_like(other)
    count = len(SLAB_STARTS)
    for j in range(pieces.shape[0]):
        lane, start = (j // count) * LANES, SLAB_STARTS[j % count]
        right[start : start + SLAB_WINDOW, lane : lane + LANES] = pieces[j]
    rows = right.shape[1]
    off = side * (rows // 2)

    def step(i):
        @pl.when(i + 1 < total)
        def _():
            begin(fetch(i + 1))

        @pl.when(i >= 2)
        def _():
            finish(away(i - 2))

        k = lax.rem(i, 2)
        _, ridx, _, nidx = columns(i, mine, 1, (idx, theirs))
        mark(ridx, marks, slice(0, ridx.shape[1]))
        t = nn(right[...], marks[...])
        tail[k] = t.astype(BF16)
        finish(fetch(i))
        query = product(head[k].astype(F32), rel[k].astype(F32))
        pos_grad = -sigmoid(-jnp.sum(query * t, axis=0, keepdims=True))
        pos_grads[i] = pos_grad
        query_low = query.astype(BF16)
        now = neg.at[k]
        negative_terms(query_low, right, now, nidx.shape[1])
        begin(away(i))
        high, low = split(pos_grad * query)
        for to, at in halves(off, rows):
            other[:, to] += nt(high, marks[at, :]) + nt(low, marks[at, :]) + nt(query_low, now[at, :]) * weights[i, :, at]

    repeat(0, total, step)
    count = len(GRAD_STARTS)
    for j in range(other_pieces.shape[0]):
        lane, start = (j // count) * LANES, GRAD_STARTS[j % count]
        other_pieces[j] = other[start : start + GRAD_WINDOW, lane : lane + LANES]

    @pl.when(total >= 2)
    def _():
        finish(away(total - 2))

    @pl.when(total >= 1)
    def _():
        finish(away(total - 1))


def left_steps(first, last, side, mine, idx, saved, own, rel_total, marks, rel_marks, bufs, sems):
    weights, pos_grads, right, *refs = saved
    rows = right.shape[1]
    off = side * (rows // 2)

    def fetch(i):
        return streams(refs, bufs, sems, i)

    @pl.when(first < last)
    def _():
        begin(fetch(first))

    def step(i):
        @pl.when(i + 1 < last)
        def _():
            begin(fetch(i + 1))

        k = lax.rem(i, 2)
        lidx, _, relx, _ = columns(i, mine, 1, idx)
        mark(lidx, marks, slice(0, lidx.shape[1]))
        finish(fetch(i))
        rel, tail, neg = [buf[k] for buf in bufs[:3]]
        query_grad = query_gradient(pos_grads[i], tail.astype(F32), right, weights[i], neg)
        high, low = split(conjugate(query_grad, rel.astype(F32)))
        for to, at in halves(off, rows):
            own[:, to] += nt(high, marks[at, :]) + nt(low, marks[at, :])
        if rel_total is not None:
            mark(relx, rel_marks, slice(0, relx.shape[1]))
            add_relations(conjugate(query_grad, bufs[3][k].astype(F32)), rel_marks, rel_total)

    repeat(first, last, step)


def left_kernel(
    counts, idx, theirs, weights, pos_grads, right, rels, tails, negs, heads, own_in, got, rel_in,
    own, keep, give, rel_total, marks, rel_marks, rel, tail, neg, head, sems,
):
    side, core, near, _ = place(counts, idx.shape[0])
    own[...] = own_in[...] + got[...]
    rel_total[...] = rel_in[...]
    left_steps(
        0, near[1], side, near[1], (idx, theirs), (weights, pos_grads, right, rels, tails, negs, heads),
        own, rel_total, marks, rel_marks, (rel, tail, neg, head), sems,
    )
    half = rel_total.shape[0] // 2
    lanes = rel_total.shape[1] // LANES

    def cut(out, first):
        for j in range(lanes):
            out[j * half : (j + 1) * half, :] = rel_total[first : first + half, j * LANES : (j + 1) * LANES]
        out[lanes * half :, :] = jnp.zeros((out.shape[0] - lanes * half, LANES), F32)

    @pl.when(core == 0)
    def _():
        cut(keep, 0)
        cut(give, half)

    @pl.when(core != 0)
    def _():
        cut(keep, half)
        cut(give, 0)


def rest_kernel(
    counts, idx, theirs, weights, pos_grads, right, rels, tails, negs, own_in, own, marks, rel, tail, neg, sems,
):
    side, _, near, every = place(counts, idx.shape[0])
    own[...] = own_in[...]
    left_steps(
        near[1], every[1], side, near[1], (idx, theirs), (weights, pos_grads, right, rels, tails, negs),
        own, None, marks, None, (rel, tail, neg), sems,
    )


def cut_kernel(slab, pieces):
    count = len(SLAB_STARTS)
    for j in range(pieces.shape[0]):
        lane, start = (j // count) * LANES, SLAB_STARTS[j % count]
        pieces[j] = slab[start : start + SLAB_WINDOW, lane : lane + LANES]


def take_kernel(matching, held, chosen, sem):
    def step(q, _):
        pltpu.make_async_copy(held.at[matching[q]], chosen.at[q], sem).start()
        return 0

    lax.fori_loop(0, held.shape[0], step, 0)
    pltpu.make_async_copy(held, chosen, sem).wait()


def put_kernel(matching, held, chosen, sem):
    def step(q, _):
        pltpu.make_async_copy(held.at[q], chosen.at[matching[q]], sem).start()
        return 0

    lax.fori_loop(0, held.shape[0], step, 0)
    pltpu.make_async_copy(held, chosen, sem).wait()


def add_kernel(own, pieces, out):
    count = len(GRAD_STARTS)
    for j in range(pieces.shape[0]):
        first, lane = GRAD_STARTS[j % count], (j // count) * LANES
        at = (slice(first, first + GRAD_WINDOW), slice(lane, lane + LANES))
        out[at] = own[at] + pieces[j]


def join_kernel(mine, theirs, out):
    side = lax.axis_index("edge")
    middle = mine.shape[1]

    @pl.when(side == 0)
    def _():
        out[:, :middle] = mine[...]
        out[:, middle:] = theirs[...]

    @pl.when(side != 0)
    def _():
        out[:, :middle] = theirs[...]
        out[:, middle:] = mine[...]


def pair_kernel(keep, got, out):
    for j in range(out.shape[0]):
        at = slice(j * REL_WINDOW, (j + 1) * REL_WINDOW)
        out[j] = keep[at, :] + got[at, :]


def sum_kernel(held, out):
    total = held[0]
    for j in range(1, held.shape[0]):
        total = total + held[j]
    out[...] = total


def spread_kernel(a, b, c, d, out):
    total = (a[...] + b[...]) + (c[...] + d[...])
    for j in range(out.shape[0]):
        out[j] = total


def close_kernel(mine, theirs, out):
    core = lax.axis_index("dom") % 2
    half, rels = out.shape[0] // 2, out.shape[1]

    def put(ref, first):
        for j in range(-(-rels // LANES)):
            lanes = min(LANES, rels - j * LANES)
            out[first : first + half, j * LANES : j * LANES + lanes] = ref[j * half : (j + 1) * half, :lanes]

    @pl.when(core == 0)
    def _():
        put(mine, 0)
        put(theirs, half)

    @pl.when(core != 0)
    def _():
        put(mine, half)
        put(theirs, 0)


def call(kernel, outs, specs, scratch, *args, flops=0, moved=0, out_specs=None):
    return pl.pallas_call(
        kernel,
        out_shape=outs,
        in_specs=specs,
        out_specs=jax.tree.map(lambda _: VM, outs) if out_specs is None else out_specs,
        scratch_shapes=scratch,
        compiler_params=PARAMS,
        cost_estimate=pl.CostEstimate(flops=flops, bytes_accessed=moved, transcendentals=0),
    )(*args)


def shape(dims, kind=F32):
    return jax.ShapeDtypeStruct(dims, kind)


def body(entities, relations, matching, group_counts, left_rows, right_rows, relation_ids, negative_rows):
    parts = lax.axis_size("dom")
    rows, width = entities.shape
    half_slots, edges = left_rows.shape[2:]
    slots = 2 * half_slots
    rels = relations.shape[0]
    padded = -(-rels // LANES) * LANES
    middle = rows // 2
    swap = [(0, 1), (1, 0)]
    plane = 2 * REL_RING
    cores = [(i, i ^ 1) for i in range(parts)]
    planes = [(i, (i + plane) % parts) for i in range(parts)]
    corners = [(2 * i + e, 2 * ((i + plane) % parts) + 1 - e) for i in range(parts) for e in range(2)]
    rings = [[z + 2 * k + c for k in range(REL_RING)] for z in range(0, parts, plane) for c in range(2)]

    def exchange(x, groups=None):
        return lax.all_to_all(x, "dom", split_axis=0, concat_axis=0, tiled=True, axis_index_groups=groups)

    packed = jnp.concatenate(
        [jnp.swapaxes(ref[0], 0, 1) for ref in (left_rows, right_rows, relation_ids, negative_rows)], axis=2
    )
    idx = (packed, lax.ppermute(packed, "edge", swap))
    slab = entities.T
    relations = relations.T
    pieces = call(cut_kernel, shape((parts, SLAB_WINDOW, LANES), BF16), [VM], [], slab)
    pieces, idx = lax.optimization_barrier((pieces, idx))
    held = exchange(pieces)

    def mem(rows_, lanes, kind=BF16):
        return pltpu.VMEM((rows_, lanes), kind)

    one_mark, two_marks, neg = mem(rows, edges), mem(rows, 2 * edges), mem(rows, edges)
    rel_marks, rel_wide = mem(padded, edges), mem(width, padded)
    two_neg = pltpu.VMEM((2, rows, edges), BF16)
    two_wide = pltpu.VMEM((2, width, edges), BF16)
    sem = pltpu.SemaphoreType.DMA

    def sems(count):
        return sem((count, 2))

    unit = 2 * width * rows * edges
    own_shape, rel_shape = shape((width, middle)), shape((width, padded))
    gathered = shape((slots, width, edges), BF16)

    heads, rel_rows, weights = call(
        gather_kernel, (gathered, gathered, shape((slots, 1, rows))), [SM] + [VM] * 4, [one_mark, rel_marks, rel_wide],
        group_counts, slab, relations, *idx, flops=13 * unit,
    )
    held, heads = lax.optimization_barrier((held, heads))
    chosen = call(take_kernel, shape(held.shape, BF16), [SM, HB], [sem], matching, held)
    partner = exchange(chosen)
    keep, give, rel_total = call(
        own_kernel, (own_shape, own_shape, rel_shape), [SM] + [VM] * 3,
        [mem(width, rows, F32), two_marks, rel_marks, neg, rel_wide],
        group_counts, slab, relations, packed, flops=40 * unit,
    )
    got = lax.ppermute(give, "edge", swap)
    other, pos_grads, right, tails, negs = call(
        right_kernel,
        (
            shape((parts, GRAD_WINDOW, LANES)),
            shape((slots, 1, edges)),
            shape((width, rows), BF16),
            gathered,
            shape((slots, rows, edges), BF16),
        ),
        [SM] + [VM] * 4 + [HB] * 2,
        [mem(width, middle, F32), one_mark, two_wide, two_wide, two_wide, two_neg, sems(2), sems(2)],
        group_counts, partner, *idx, weights, heads, rel_rows,
        flops=30 * unit, out_specs=(VM, VM, VM, HB, HB),
    )
    grad_held = exchange(other)
    rel_flat = shape((REL_RING * REL_WINDOW, LANES))
    saved = (weights, pos_grads, right, rel_rows, tails, negs)
    own, rel_keep, rel_give = call(
        left_kernel, (own_shape, rel_flat, rel_flat), [SM] + [VM] * 5 + [HB] * 4 + [VM] * 3,
        [mem(width, padded, F32), one_mark, rel_marks, two_wide, two_wide, two_neg, two_wide, sems(4)],
        group_counts, *idx, *saved, heads, keep, got, rel_total, flops=20 * unit,
    )
    rel_got = lax.ppermute(rel_give, "dom", cores)
    grad_chosen = call(put_kernel, shape(grad_held.shape), [SM, VM], [sem], matching, grad_held, out_specs=HB)
    rel_keep, _ = lax.optimization_barrier((rel_keep, grad_chosen))
    rel_pieces = call(pair_kernel, shape((REL_RING, REL_WINDOW, LANES)), [VM, VM], [], rel_keep, rel_got)
    rel_held = exchange(rel_pieces, rings)
    rel_sum = call(sum_kernel, shape((REL_WINDOW, LANES)), [VM], [], rel_held)
    rel_held, grad_chosen = lax.optimization_barrier((rel_held, grad_chosen))
    grad_pieces = exchange(grad_chosen)
    rel_sums = [rel_sum, lax.ppermute(rel_sum, "dom", planes), lax.ppermute(rel_sum, "edge", swap)]
    rel_sums += [lax.ppermute(rel_sum, ("dom", "edge"), corners)]
    own, _ = lax.optimization_barrier((own, rel_sum))
    own = call(
        rest_kernel, own_shape, [SM] + [VM] * 5 + [HB] * 3 + [VM], [one_mark, two_wide, two_wide, two_neg, sems(3)],
        group_counts, *idx, *saved, own, flops=15 * unit,
    )
    own, grad_pieces, rel_sums = lax.optimization_barrier((own, grad_pieces, rel_sums))
    half = call(add_kernel, own_shape, [VM] * 2, [], own, grad_pieces)
    far = lax.ppermute(half, "edge", swap)
    rel_sums, half = lax.optimization_barrier((rel_sums, half))
    rel_full = call(spread_kernel, shape(rel_pieces.shape), [VM] * 4, [], *rel_sums)
    rel_mine = exchange(rel_full, rings).reshape(rel_flat.shape)
    rel_far = lax.ppermute(rel_mine, "dom", cores)
    relation_grad = call(close_kernel, shape((width, rels)), [VM, VM], [], rel_mine, rel_far)
    total = call(join_kernel, shape((width, rows)), [VM, VM], [], half, far)
    return total.T, relation_grad.T


def solution(mesh):
    placed = (
        P("dom", None),
        P(),
        P(),
        P("dom", None),
        P("dom", None, "edge", None),
        P("dom", None, "edge", None),
        P("dom", None, "edge", None),
        P("dom", None, "edge", None),
    )
    return jax.shard_map(
        body, mesh=mesh, in_specs=placed, out_specs=(P("dom", None), P()), check_vma=False
    )
```

time: 442 us -> 286 us (0.65)
  waiting for transfers between devices: 224 us -> 71 us
  blocking collectives: 71.4 us -> 22.1 us
  starting transfers between devices: 27.2 us -> 63.6 us
  Pallas kernels: 85.4 us -> 117 us
  between operations: 15 us -> 0.83 us
    psum x1 -> x0, waiting for transfers between devices: 120 us -> none  [body(): relation_grad = lax.psum(rel_part, ('dom', 'edge'))]
    ppermute x1, waiting for transfers between devices: 55.8 us -> 0.01 us  [body(): got = lax.ppermute(give, 'edge', swap)]
    all_to_all x1, blocking collectives: 71.4 us -> 22.1 us  [exchange(): lax.all_to_all(x, 'dom', split_axis=0, concat_axis=0, tiled=True, axis_in...]
    pallas_call x8 -> x14, Pallas kernels: 85.4 us -> 117 us  [call(): pl.pallas_call(kernel, out_shape=outs, in_specs=specs, out_specs=jax.tree...]
    all_to_all x3 -> x5, starting transfers between devices: 23.6 us -> 50.7 us  [exchange(): lax.all_to_all(x, 'dom', split_axis=0, concat_axis=0, tiled=True, axis_in...]
    all_to_all x3 -> x5, waiting for transfers between devices: 8.88 us -> 35.2 us  [exchange(): lax.all_to_all(x, 'dom', split_axis=0, concat_axis=0, tiled=True, axis_in...]
    ppermute x1 -> x7, starting transfers between devices: 1.86 us -> 12.9 us  [the longest x1 4.5 us: body(): idx = (packed, lax.ppermute(packed, 'edge', swap))]
    ppermute x1 -> x7, waiting for transfers between devices: 39.2 us -> 35.8 us  [the longest x1 17.8 us: body(): far = lax.ppermute(half, 'edge', swap)]
  transfers between devices with their start and end apart: 6 -> 13, of which waited for: 5 -> 6; matrix products, arithmetic and copies ran while one was open for 2% -> 0% of each run, Pallas kernels for 9% -> 36%
where the time goes in v2:
time: 286 us; the launch traced here: 285 us
  Pallas kernels  117 us (41%)
  waiting for transfers between devices  71 us (25%)
  starting transfers between devices  63.6 us (22%)
  blocking collectives  22.1 us (8%)
  local copies, waits for them, and re-layouts  8.85 us (3%)
    pallas_call x14, Pallas kernels, call(): pl.pallas_call(kernel, out_shape=outs, in_specs=specs, out_specs=jax.tree...  117 us
    all_to_all x5, starting transfers between devices, exchange(): lax.all_to_all(x, 'dom', split_axis=0, concat_axis=0, tiled=True, axis_in...  50.7 us
    all_to_all x5, waiting for transfers between devices, exchange(): lax.all_to_all(x, 'dom', split_axis=0, concat_axis=0, tiled=True, axis_in...  35.2 us
    all_to_all x1, blocking collectives, exchange(): lax.all_to_all(x, 'dom', split_axis=0, concat_axis=0, tiled=True, axis_in...  22.1 us
    ppermute x1, waiting for transfers between devices, body(): far = lax.ppermute(half, 'edge', swap)  17.8 us
    ppermute x1, waiting for transfers between devices, body(): lax.ppermute(rel_sum, 'edge', swap)  15 us
    unnamed x28, local copies, waits for them, and re-layouts  8.85 us
  transfers between devices with their start and end apart: 13, of which 6 were waited for; matrix products, arithmetic and copies ran while one was open for 0% of the time, Pallas kernels for 36%

profile of v2, /device:TPU:1, one launch (start us, length us, event | category | flops | bytes accessed | tf_op | source)
XLA Modules:
  0.0 284.5 jit_solution(15136453333630348299)
XLA Ops:
  1.4 4.5 %collective-permute-start = (s32[3,2,2560]{2,1,0:T(2,128)S(1)}, s32[3,2,2560]{2,1,0:T(2,128)S(1)}, u32[]{:S(2)}, u32[]{:S(2)}) collective-permute-start(s32[3,2,2560]{2,1,0:T(2,128)S(1)} %pad_add_fusion.idx), channel_id=1, source_target_pairs={{0,1},{1,0},{2,3},{3,2},{4,5},{5,4},{6,7},{7,6},{8,9},{9,8},{10,11... | collective-permute-start | bytes 184328 | tf_op jit(solution)/shard_map/ppermute | solution.py:474
  5.9 3.0 %shard_map.95 = bf16[64,112,128]{2,1,0:T(8,128)(2,1)} custom-call(bf16[400,2048]{1,0:T(8,128)(2,1)} %bitcast.21), custom_call_target="tpu_custom_call" | custom-call | tf_op jit(solution)/shard_map/pallas_call | solution.py:438
  9.5 8.9 %all-to-all-start = ((bf16[64,112,128]{2,1,0:T(8,128)(2,1)}), bf16[64,112,128]{2,1,0:T(8,128)(2,1)S(1)}, u32[]{:S(2)}, u32[]{:S(2)}) async-start(bf16[64,112,128]{2,1,0:T(8,128)(2,1)} %shard_map.95), calls=%async_computation | async-start | bytes 3670016 | tf_op jit(solution)/shard_map/all_to_all | solution.py:469
  18.4 9.3 %shard_map.96 = (bf16[6,400,512]{2,1,0:T(8,128)(2,1)}, bf16[6,400,512]{2,1,0:T(8,128)(2,1)}, f32[6,1,2048]{2,1,0:T(1,128)}) custom-call(s32[1,2]{1,0:T(1,128)} %counts.9, bf16[400,2048]{1,0:T(8,128)(2,1)} %bitcast.22, bf16[400,1345]{1,0:T(8,128)(2,1)} %bitcast.28, s32[3,2,2560]{2,1,0:T(2,128)} %copy-done.11, s32[3,2,2560]{2,1,0:T(2,128)} %copy-done.13), custom_call_target="tpu_custom_call" | custom-call | flops 10905190400 | tf_op jit(solution)/shard_map/pallas_call | solution.py:438
  27.7 16.3 %all-to-all-done.held = bf16[64,112,128]{2,1,0:T(8,128)(2,1)S(1)} async-done(((bf16[64,112,128]{2,1,0:T(8,128)(2,1)}), bf16[64,112,128]{2,1,0:T(8,128)(2,1)S(1)}, u32[]{:S(2)}, u32[]{:S(2)}) %all-to-all-start) | async-done | bytes 1835040 | tf_op jit(solution)/shard_map/all_to_all | solution.py:469
  45.2 3.4 %shard_map.97 = bf16[64,112,128]{2,1,0:T(8,128)(2,1)} custom-call(s32[64]{0:T(128)} %matching.3, bf16[64,112,128]{2,1,0:T(8,128)(2,1)} %copy-done.2), custom_call_target="tpu_custom_call" | custom-call | tf_op jit(solution)/shard_map/pallas_call | solution.py:438
  48.6 5.1 %all-to-all-start.1 = ((bf16[64,112,128]{2,1,0:T(8,128)(2,1)}), bf16[64,112,128]{2,1,0:T(8,128)(2,1)S(1)}, u32[]{:S(2)}, u32[]{:S(2)}) async-start(bf16[64,112,128]{2,1,0:T(8,128)(2,1)} %shard_map.97), calls=%async_computation.1 | async-start | bytes 3670016 | tf_op jit(solution)/shard_map/all_to_all | solution.py:469
  53.8 39.2 %shard_map.99 = (f32[400,1024]{1,0:T(8,128)}, f32[400,1024]{1,0:T(8,128)}, f32[400,1408]{1,0:T(8,128)}) custom-call(s32[1,2]{1,0:T(1,128)} %counts.9, bf16[400,2048]{1,0:T(8,128)(2,1)} %bitcast.23, bf16[400,1345]{1,0:T(8,128)(2,1)} %bitcast.29, s32[3,2,2560]{2,1,0:T(2,128)} %copy-done.11), custom_call_target="tpu_custom_call" | custom-call | flops 33554432000 | tf_op jit(solution)/shard_map/pallas_call | solution.py:438
  94.3 18.4 %shard_map.98 = (f32[64,56,128]{2,1,0:T(8,128)}, f32[6,1,512]{2,1,0:T(1,128)}, bf16[400,2048]{1,0:T(8,128)(2,1)}, bf16[6,400,512]{2,1,0:T(8,128)(2,1)}, bf16[6,2048,512]{2,1,0:T(8,128)(2,1)}) custom-call(s32[1,2]{1,0:T(1,128)} %counts.9, bf16[64,112,128]{2,1,0:T(8,128)(2,1)} %copy-done.5, s32[3,2,2560]{2,1,0:T(2,128)} %copy-done.11, ...), custom_call_target="tpu_custom_call" | custom-call | flops 25165824000 | tf_op jit(solution)/shard_map/pallas_call | solution.py:438
  112.7 24.7 %all-to-all-start.2 = ((f32[64,56,128]{2,1,0:T(8,128)}), f32[64,56,128]{2,1,0:T(8,128)S(1)}, u32[]{:S(2)}, u32[]{:S(2)}) async-start(f32[64,56,128]{2,1,0:T(8,128)} %get-tuple-element.52), calls=%async_computation.2 | async-start | bytes 3670016 | tf_op jit(solution)/shard_map/all_to_all | solution.py:469
  138.5 20.6 %shard_map.100 = (f32[400,1024]{1,0:T(8,128)}, f32[2304,128]{1,0:T(8,128)}, f32[2304,128]{1,0:T(8,128)}) custom-call(s32[1,2]{1,0:T(1,128)} %counts.9, s32[3,2,2560]{2,1,0:T(2,128)} %copy-done.11, s32[3,2,2560]{2,1,0:T(2,128)} %copy-done.13, f32[6,1,2048]{2,1,0:T(1,128)} %get-tuple-element.37.weights, f32[6,1,512]{2,1,0:T(1,128)} %get-tuple-element.43.pos_grads, ...), custom_call_target="tpu_custom_call" | custom-call | flops 16777216000 | tf_op jit(solution)/shard_map/pallas_call | solution.py:438
  159.2 3.7 %all-to-all-done.2.held = f32[64,56,128]{2,1,0:T(8,128)S(1)} async-done(((f32[64,56,128]{2,1,0:T(8,128)}), f32[64,56,128]{2,1,0:T(8,128)S(1)}, u32[]{:S(2)}, u32[]{:S(2)}) %all-to-all-start.2) | async-done | bytes 1835040 | tf_op jit(solution)/shard_map/all_to_all | solution.py:469
  170.7 22.1 %all_to_all.30.held = f32[16,144,128]{2,1,0:T(8,128)} all-to-all(f32[16,144,128]{2,1,0:T(8,128)} %shard_map.102), channel_id=1, replica_groups={{0,4,8,12,16,20,24,28,32,36,40,44,48,52,56,60},{2,6,10,14,18,22,26,30,3..., dimensions={0} | all-to-all | bytes 2359296 | tf_op jit(solution)/shard_map/all_to_all | solution.py:469
  192.7 6.8 %all-to-all-start.4 = ((f32[64,56,128]{2,1,0:T(8,128)}), f32[64,56,128]{2,1,0:T(8,128)S(1)}, u32[]{:S(2)}, u32[]{:S(2)}) async-start(f32[64,56,128]{2,1,0:T(8,128)} %shard_map.101), calls=%async_computation.4 | async-start | bytes 3670016 | tf_op jit(solution)/shard_map/all_to_all | solution.py:469
  204.8 3.4 %shard_map.104.own = f32[400,1024]{1,0:T(8,128)} custom-call(s32[1,2]{1,0:T(1,128)} %counts.9, s32[3,2,2560]{2,1,0:T(2,128)} %copy-done.11, s32[3,2,2560]{2,1,0:T(2,128)} %copy-done.13, f32[6,1,2048]{2,1,0:T(1,128)} %get-tuple-element.37.weights, f32[6,1,512]{2,1,0:T(1,128)} %get-tuple-element.43.pos_grads, bf16[400,2048]{1,0:T(8,128)(2,1)} %get-tuple-element.44.right, ...), custom_call_target="tpu_custom_call" | custom-call | flops 12582912000 | tf_op jit(solution)/shard_map/pallas_call | solution.py:438
  208.2 15.0 %collective-permute-done.4.c = f32[144,128]{1,0:T(8,128)S(1)} collective-permute-done((f32[144,128]{1,0:T(8,128)}, f32[144,128]{1,0:T(8,128)S(1)}, u32[]{:S(2)}, u32[]{:S(2)}) %collective-permute-start.4) | collective-permute-done | bytes 73760 | tf_op jit(solution)/shard_map/ppermute | solution.py:540
  223.2 2.9 %collective-permute-done.3.b = f32[144,128]{1,0:T(8,128)S(1)} collective-permute-done((f32[144,128]{1,0:T(8,128)}, f32[144,128]{1,0:T(8,128)S(1)}, u32[]{:S(2)}, u32[]{:S(2)}) %collective-permute-start.3) | collective-permute-done | bytes 73760 | tf_op jit(solution)/shard_map/ppermute | solution.py:540
  227.4 3.5 %shard_map.105.mine = f32[400,1024]{1,0:T(8,128)} custom-call(f32[400,1024]{1,0:T(8,128)} %shard_map.104.own, f32[64,56,128]{2,1,0:T(8,128)} %copy-done), custom_call_target="tpu_custom_call" | custom-call | tf_op jit(solution)/shard_map/pallas_call | solution.py:438
  233.2 5.2 %all-to-all-start.5 = ((f32[16,144,128]{2,1,0:T(8,128)}), f32[16,144,128]{2,1,0:T(8,128)S(1)}, u32[]{:S(2)}, u32[]{:S(2)}) async-start(f32[16,144,128]{2,1,0:T(8,128)} %shard_map.107), calls=%async_computation.5 | async-start | bytes 2359296 | tf_op jit(solution)/shard_map/all_to_all | solution.py:469
  240.0 15.2 %all-to-all-done.5 = f32[16,144,128]{2,1,0:T(8,128)S(1)} async-done(((f32[16,144,128]{2,1,0:T(8,128)}), f32[16,144,128]{2,1,0:T(8,128)S(1)}, u32[]{:S(2)}, u32[]{:S(2)}) %all-to-all-start.5) | async-done | bytes 1179680 | tf_op jit(solution)/shard_map/all_to_all | solution.py:469
  255.2 3.4 %collective-permute-start.7 = (f32[2304,128]{1,0:T(8,128)S(1)}, f32[2304,128]{1,0:T(8,128)S(1)}, u32[]{:S(2)}, u32[]{:S(2)}) collective-permute-start(f32[2304,128]{1,0:T(8,128)S(1)} %bitcast.17), channel_id=1, source_target_pairs={{0,2},{2,0},{4,6},{6,4},{8,10},{10,8},{12,14},{14,12},{16,18},{18,... | collective-permute-start | bytes 3538952 | tf_op jit(solution)/shard_map/ppermute | solution.py:553
  258.6 17.8 %collective-permute-done.6.theirs = f32[400,1024]{1,0:T(8,128)} collective-permute-done((f32[400,1024]{1,0:T(8,128)S(1)}, f32[400,1024]{1,0:T(8,128)}, u32[]{:S(2)}, u32[]{:S(2)}) %collective-permute-start.6) | collective-permute-done | bytes 1638432 | tf_op jit(solution)/shard_map/ppermute | solution.py:549
  276.5 3.8 %shard_map.106 = f32[400,2048]{1,0:T(8,128)} custom-call(f32[400,1024]{1,0:T(8,128)} %shard_map.105.mine, f32[400,1024]{1,0:T(8,128)} %collective-permute-done.6.theirs), custom_call_target="tpu_custom_call" | custom-call | tf_op jit(solution)/shard_map/pallas_call | solution.py:438
  281.4 3.1 %shard_map.108 = f32[400,1345]{1,0:T(8,128)} custom-call(f32[2304,128]{1,0:T(8,128)} %bitcast.18, f32[2304,128]{1,0:T(8,128)} %copy-done.7), custom_call_target="tpu_custom_call" | custom-call | tf_op jit(solution)/shard_map/pallas_call | solution.py:438
  (46 shorter events, 24.3 us)
Async XLA Ops:
  1.4 7.5 %copy-start.11 = (s32[3,2,2560]{2,1,0:T(2,128)}, s32[3,2,2560]{2,1,0:T(2,128)S(1)}, u32[]{:S(2)}) copy-start(s32[3,2,2560]{2,1,0:T(2,128)S(1)} %pad_add_fusion.idx) | copy-start | bytes 184324
  1.4 7.5 %collective-permute-start = (s32[3,2,2560]{2,1,0:T(2,128)S(1)}, s32[3,2,2560]{2,1,0:T(2,128)S(1)}, u32[]{:S(2)}, u32[]{:S(2)}) collective-permute-start(s32[3,2,2560]{2,1,0:T(2,128)S(1)} %pad_add_fusion.idx), channel_id=1, source_target_pairs={{0,1},{1,0},{2,3},{3,2},{4,5},{5,4},{6,7},{7,6},{8,9},{9,8},{10,11... | collective-permute-start | bytes 184328 | tf_op jit(solution)/shard_map/ppermute | solution.py:474
  9.5 34.5 %all-to-all-start = ((bf16[64,112,128]{2,1,0:T(8,128)(2,1)}), bf16[64,112,128]{2,1,0:T(8,128)(2,1)S(1)}, u32[]{:S(2)}, u32[]{:S(2)}) async-start(bf16[64,112,128]{2,1,0:T(8,128)(2,1)} %shard_map.95), calls=%async_computation | async-start | bytes 3670016 | tf_op jit(solution)/shard_map/all_to_all | solution.py:469
  44.0 1.2 copy-start.2
  48.6 44.4 %all-to-all-start.1 = ((bf16[64,112,128]{2,1,0:T(8,128)(2,1)}), bf16[64,112,128]{2,1,0:T(8,128)(2,1)S(1)}, u32[]{:S(2)}, u32[]{:S(2)}) async-start(bf16[64,112,128]{2,1,0:T(8,128)(2,1)} %shard_map.97), calls=%async_computation.1 | async-start | bytes 3670016 | tf_op jit(solution)/shard_map/all_to_all | solution.py:469
  93.0 44.4 %collective-permute-start.1 = (f32[400,1024]{1,0:T(8,128)}, f32[400,1024]{1,0:T(8,128)S(1)}, u32[]{:S(2)}, u32[]{:S(2)}) collective-permute-start(f32[400,1024]{1,0:T(8,128)} %get-tuple-element.48), channel_id=1, source_target_pairs={{0,1},{1,0},{2,3},{3,2},{4,5},{5,4},{6,7},{7,6},{8,9},{9,8},{10,11... | collective-permute-start | bytes 4915208 | tf_op jit(solution)/shard_map/ppermute | solution.py:509
  93.0 1.3 copy-start.5
  112.7 50.3 %all-to-all-start.2 = ((f32[64,56,128]{2,1,0:T(8,128)}), f32[64,56,128]{2,1,0:T(8,128)S(1)}, u32[]{:S(2)}, u32[]{:S(2)}) async-start(f32[64,56,128]{2,1,0:T(8,128)} %get-tuple-element.52), calls=%async_computation.2 | async-start | bytes 3670016 | tf_op jit(solution)/shard_map/all_to_all | solution.py:469
  137.3 1.2 copy-start.12
  159.1 7.7 %collective-permute-start.2 = (f32[2304,128]{1,0:T(8,128)}, f32[2304,128]{1,0:T(8,128)S(1)}, u32[]{:S(2)}, u32[]{:S(2)}) collective-permute-start(f32[2304,128]{1,0:T(8,128)} %get-tuple-element.54), channel_id=1, source_target_pairs={{0,2},{2,0},{4,6},{6,4},{8,10},{10,8},{12,14},{14,12},{16,18},{18,... | collective-permute-start | bytes 3538952 | tf_op jit(solution)/shard_map/ppermute | solution.py:532
  162.9 1.2 copy-start.1
  192.7 33.4 %all-to-all-start.4 = ((f32[64,56,128]{2,1,0:T(8,128)}), f32[64,56,128]{2,1,0:T(8,128)S(1)}, u32[]{:S(2)}, u32[]{:S(2)}) async-start(f32[64,56,128]{2,1,0:T(8,128)} %shard_map.101), calls=%async_computation.4 | async-start | bytes 3670016 | tf_op jit(solution)/shard_map/all_to_all | solution.py:469
  201.5 6.7 %collective-permute-start.5 = (f32[144,128]{1,0:T(8,128)}, f32[144,128]{1,0:T(8,128)S(1)}, u32[]{:S(2)}, u32[]{:S(2)}) collective-permute-start(f32[144,128]{1,0:T(8,128)} %shard_map.103.a), channel_id=1, source_target_pairs={{0,65},{1,64},{2,67},{3,66},{4,69},{5,68},{6,71},{7,70},{8,73},{9,... | collective-permute-start | bytes 221192 | tf_op jit(solution)/shard_map/ppermute | solution.py:541
  202.9 20.3 %collective-permute-start.4 = (f32[144,128]{1,0:T(8,128)}, f32[144,128]{1,0:T(8,128)S(1)}, u32[]{:S(2)}, u32[]{:S(2)}) collective-permute-start(f32[144,128]{1,0:T(8,128)} %shard_map.103.a), channel_id=1, source_target_pairs={{0,1},{1,0},{2,3},{3,2},{4,5},{5,4},{6,7},{7,6},{8,9},{9,8},{10,11... | collective-permute-start | bytes 221192 | tf_op jit(solution)/shard_map/ppermute | solution.py:540
  204.8 21.4 %collective-permute-start.3 = (f32[144,128]{1,0:T(8,128)}, f32[144,128]{1,0:T(8,128)S(1)}, u32[]{:S(2)}, u32[]{:S(2)}) collective-permute-start(f32[144,128]{1,0:T(8,128)} %shard_map.103.a), channel_id=1, source_target_pairs={{0,64},{2,66},{4,68},{6,70},{8,72},{10,74},{12,76},{14,78},{16,80}... | collective-permute-start | bytes 221192 | tf_op jit(solution)/shard_map/ppermute | solution.py:540
  208.2 22.7 %copy-start.8 = (f32[144,128]{1,0:T(8,128)}, f32[144,128]{1,0:T(8,128)S(1)}, u32[]{:S(2)}) copy-start(f32[144,128]{1,0:T(8,128)S(1)} %collective-permute-done.5.d) | copy-start | bytes 221188
  223.2 7.7 %copy-start.9 = (f32[144,128]{1,0:T(8,128)}, f32[144,128]{1,0:T(8,128)S(1)}, u32[]{:S(2)}) copy-start(f32[144,128]{1,0:T(8,128)S(1)} %collective-permute-done.4.c) | copy-start | bytes 221188
  226.2 4.8 %copy-start.10 = (f32[144,128]{1,0:T(8,128)}, f32[144,128]{1,0:T(8,128)S(1)}, u32[]{:S(2)}) copy-start(f32[144,128]{1,0:T(8,128)S(1)} %collective-permute-done.3.b) | copy-start | bytes 221188
  226.2 1.2 copy-start
  230.9 7.4 %copy-start.3 = (f32[400,1024]{1,0:T(8,128)S(1)}, f32[400,1024]{1,0:T(8,128)}, u32[]{:S(2)}) copy-start(f32[400,1024]{1,0:T(8,128)} %shard_map.105.mine) | copy-start | bytes 4915204
  233.2 22.1 %all-to-all-start.5 = ((f32[16,144,128]{2,1,0:T(8,128)}), f32[16,144,128]{2,1,0:T(8,128)S(1)}, u32[]{:S(2)}, u32[]{:S(2)}) async-start(f32[16,144,128]{2,1,0:T(8,128)} %shard_map.107), calls=%async_computation.5 | async-start | bytes 2359296 | tf_op jit(solution)/shard_map/all_to_all | solution.py:469
  238.4 38.1 %collective-permute-start.6 = (f32[400,1024]{1,0:T(8,128)S(1)}, f32[400,1024]{1,0:T(8,128)}, u32[]{:S(2)}, u32[]{:S(2)}) collective-permute-start(f32[400,1024]{1,0:T(8,128)S(1)} %copy-done.3), channel_id=1, source_target_pairs={{0,1},{1,0},{2,3},{3,2},{4,5},{5,4},{6,7},{7,6},{8,9},{9,8},{10,11... | collective-permute-start | bytes 4915208 | tf_op jit(solution)/shard_map/ppermute | solution.py:549
  255.2 25.1 %copy-start.4 = (f32[16,144,128]{2,1,0:T(8,128)}, f32[16,144,128]{2,1,0:T(8,128)S(1)}, u32[]{:S(2)}) copy-start(f32[16,144,128]{2,1,0:T(8,128)S(1)} %all-to-all-done.5) | copy-start | bytes 3538948
  255.2 25.1 %collective-permute-start.7 = (f32[2304,128]{1,0:T(8,128)S(1)}, f32[2304,128]{1,0:T(8,128)S(1)}, u32[]{:S(2)}, u32[]{:S(2)}) collective-permute-start(f32[2304,128]{1,0:T(8,128)S(1)} %bitcast.17), channel_id=1, source_target_pairs={{0,2},{2,0},{4,6},{6,4},{8,10},{10,8},{12,14},{14,12},{16,18},{18,... | collective-permute-start | bytes 3538952 | tf_op jit(solution)/shard_map/ppermute | solution.py:553
  (3 other events, 2.7 us)

commit v3 on v2

--- a/solution.py
+++ b/solution.py
@@ -11,7 +11,7 @@
 VM = pl.BlockSpec(memory_space=pltpu.VMEM)
 SM = pl.BlockSpec(memory_space=pltpu.SMEM)
 HB = pl.BlockSpec(memory_space=pl.ANY)
-PARAMS = pltpu.CompilerParams(vmem_limit_bytes=58 * 2**20)
+PARAMS = pltpu.CompilerParams(vmem_limit_bytes=63 * 2**20)
 
 LANES = 128
 SLAB_WINDOW = 112
@@ -106,17 +106,14 @@
     rel_total[...] += nt(high, rel_marks[...]) + nt(low, rel_marks[...])
 
 
-def own_slot(position, slab, relations, idx, own, rel_total, marks, rel_marks, neg):
+def own_slot(position, slab, idx, own, rel_total, marks, rel_marks, neg, gathered):
     lidx, ridx, relx, nidx = columns(position, 0, 0, (idx, None))
     edges, negatives = lidx.shape[1], nidx.shape[1]
     rows = slab.shape[1]
-    left_lanes, right_lanes = slice(0, edges), slice(edges, 2 * edges)
-    mark(lidx, marks, left_lanes)
-    mark(ridx, marks, right_lanes)
+    mark(lidx, marks, slice(0, edges))
+    mark(ridx, marks, slice(edges, 2 * edges))
     mark(relx, rel_marks, slice(0, edges))
-    h = nn(slab[...], marks[:, left_lanes])
-    t = nn(slab[...], marks[:, right_lanes])
-    rel = nn(relations[...], rel_marks[...])
+    h, rel, t = [x.astype(F32) for x in gathered()]
     query = product(h, rel)
     pos_grad = -sigmoid(-jnp.sum(query * t, axis=0, keepdims=True))
     query_low = query.astype(BF16)
@@ -173,9 +170,23 @@
         copy.wait()
 
 
-def gather_kernel(counts, slab, relations, idx, theirs, heads, rels, weights, marks, rel_marks, rel_wide):
+def gather_kernel(
+    counts, slab, relations, idx, theirs,
+    heads, rels, weights, own_heads, own_rels, own_tails, marks, rel_marks, rel_wide,
+):
     _, _, near, every = place(counts, idx.shape[0])
     widen(relations, rel_wide)
+
+    def own_step(i):
+        lidx, ridx, relx, _ = columns(i, 0, 0, (idx, None))
+        mark(lidx, marks, slice(0, lidx.shape[1]))
+        mark(relx, rel_marks, slice(0, relx.shape[1]))
+        own_heads[i] = nn(slab[...], marks[...]).astype(BF16)
+        own_rels[i] = nn(rel_wide[...], rel_marks[...]).astype(BF16)
+        mark(ridx, marks, slice(0, ridx.shape[1]))
+        own_tails[i] = nn(slab[...], marks[...]).astype(BF16)
+
+    repeat(0, near[0], own_step)
 
     def step(i):
         lidx, _, relx, nidx = columns(i, near[1], 1, (idx, theirs))
@@ -188,12 +199,35 @@
     repeat(0, every[1], step)
 
 
-def own_kernel(counts, slab, relations, idx, keep, give, rel_total, own, marks, rel_marks, neg, rel_wide):
+def own_kernel(
+    counts, slab, idx, heads, rels, tails,
+    keep, give, rel_total, own, marks, rel_marks, neg, head, rel, tail, sems,
+):
     side, _, near, _ = place(counts, idx.shape[0])
+    last = near[0]
+
+    def fetch(i):
+        return streams((heads, rels, tails), (head, rel, tail), sems, i)
+
+    @pl.when(last >= 1)
+    def _():
+        begin(fetch(0))
+
     own[...] = jnp.zeros_like(own)
     rel_total[...] = jnp.zeros_like(rel_total)
-    widen(relations, rel_wide)
-    repeat(0, near[0], lambda i: own_slot(i, slab, rel_wide, idx, own, rel_total, marks, rel_marks, neg))
+
+    def step(i):
+        @pl.when(i + 1 < last)
+        def _():
+            begin(fetch(i + 1))
+
+        def gathered():
+            finish(fetch(i))
+            return [buf[lax.rem(i, 2)] for buf in (head, rel, tail)]
+
+        own_slot(i, slab, idx, own, rel_total, marks, rel_marks, neg, gathered)
+
+    repeat(0, last, step)
     middle = keep.shape[1]
 
     @pl.when(side == 0)
@@ -307,11 +341,11 @@
 
 
 def left_kernel(
-    counts, idx, theirs, weights, pos_grads, right, rels, tails, negs, heads, own_in, got, rel_in,
+    counts, idx, theirs, weights, pos_grads, right, rels, tails, negs, heads, far_own, rel_in,
     own, keep, give, rel_total, marks, rel_marks, rel, tail, neg, head, sems,
 ):
     side, core, near, _ = place(counts, idx.shape[0])
-    own[...] = own_in[...] + got[...]
+    own[...] = jnp.zeros_like(own)
     rel_total[...] = rel_in[...]
     left_steps(
         0, near[1], side, near[1], (idx, theirs), (weights, pos_grads, right, rels, tails, negs, heads),
@@ -337,10 +371,10 @@
 
 
 def rest_kernel(
-    counts, idx, theirs, weights, pos_grads, right, rels, tails, negs, own_in, own, marks, rel, tail, neg, sems,
+    counts, idx, theirs, weights, pos_grads, right, rels, tails, negs, own_in, near_own, far_own, own, marks, rel, tail, neg, sems,
 ):
     side, _, near, every = place(counts, idx.shape[0])
-    own[...] = own_in[...]
+    own[...] = own_in[...] + (near_own[...] + far_own[...])
     left_steps(
         near[1], every[1], side, near[1], (idx, theirs), (weights, pos_grads, right, rels, tails, negs),
         own, None, marks, None, (rel, tail, neg), sems,
@@ -372,27 +406,52 @@
     pltpu.make_async_copy(held, chosen, sem).wait()
 
 
-def add_kernel(own, pieces, out):
-    count = len(GRAD_STARTS)
+def add_kernel(own, pieces, first, second):
+    count, cut = len(GRAD_STARTS), first.shape[0]
     for j in range(pieces.shape[0]):
-        first, lane = GRAD_STARTS[j % count], (j // count) * LANES
-        at = (slice(first, first + GRAD_WINDOW), slice(lane, lane + LANES))
-        out[at] = own[at] + pieces[j]
-
-
-def join_kernel(mine, theirs, out):
+        start, lane = GRAD_STARTS[j % count], (j // count) * LANES
+        lanes = slice(lane, lane + LANES)
+        total = own[start : start + GRAD_WINDOW, lanes] + pieces[j]
+        here = max(0, min(cut - start, GRAD_WINDOW))
+        if here:
+            first[start : start + here, lanes] = total[:here]
+        if here < GRAD_WINDOW:
+            second[start + here - cut : start + GRAD_WINDOW - cut, lanes] = total[here:]
+
+
+def write(parts, sems):
+    copies = [pltpu.make_async_copy(a, b, sems.at[n, 0]) for n, (a, b) in enumerate(parts)]
+    begin(copies)
+    finish(copies)
+
+
+def join_kernel(first, second, far, out, sems):
     side = lax.axis_index("edge")
-    middle = mine.shape[1]
+    middle, cut = first.shape[1], first.shape[0]
+
+    def put(near, away):
+        write([(first, out.at[:cut, near]), (second, out.at[cut:, near]), (far, out.at[:cut, away])], sems)
 
     @pl.when(side == 0)
     def _():
-        out[:, :middle] = mine[...]
-        out[:, middle:] = theirs[...]
+        put(slice(0, middle), slice(middle, 2 * middle))
 
     @pl.when(side != 0)
     def _():
-        out[:, :middle] = theirs[...]
-        out[:, middle:] = mine[...]
+        put(slice(middle, 2 * middle), slice(0, middle))
+
+
+def last_kernel(begun, far, out, sems):
+    side = lax.axis_index("edge")
+    middle, cut = far.shape[1], out.shape[0] - far.shape[0]
+
+    @pl.when(side == 0)
+    def _():
+        write([(far, out.at[cut:, middle:])], sems)
+
+    @pl.when(side != 0)
+    def _():
+        write([(far, out.at[cut:, :middle])], sems)
 
 
 def pair_kernel(keep, got, out):
@@ -434,7 +493,7 @@
         put(theirs, 0)
 
 
-def call(kernel, outs, specs, scratch, *args, flops=0, moved=0, out_specs=None):
+def call(kernel, outs, specs, scratch, *args, flops=0, moved=0, out_specs=None, aliases={}):
     return pl.pallas_call(
         kernel,
         out_shape=outs,
@@ -442,6 +501,7 @@
         out_specs=jax.tree.map(lambda _: VM, outs) if out_specs is None else out_specs,
         scratch_shapes=scratch,
         compiler_params=PARAMS,
+        input_output_aliases=aliases,
         cost_estimate=pl.CostEstimate(flops=flops, bytes_accessed=moved, transcendentals=0),
     )(*args)
 
@@ -494,17 +554,19 @@
     own_shape, rel_shape = shape((width, middle)), shape((width, padded))
     gathered = shape((slots, width, edges), BF16)
 
-    heads, rel_rows, weights = call(
-        gather_kernel, (gathered, gathered, shape((slots, 1, rows))), [SM] + [VM] * 4, [one_mark, rel_marks, rel_wide],
-        group_counts, slab, relations, *idx, flops=13 * unit,
+    near_gathered = shape((half_slots, width, edges), BF16)
+    heads, rel_rows, weights, *own_rows = call(
+        gather_kernel, (gathered, gathered, shape((slots, 1, rows))) + (near_gathered,) * 3,
+        [SM] + [VM] * 4, [one_mark, rel_marks, rel_wide],
+        group_counts, slab, relations, *idx, flops=22 * unit,
     )
     held, heads = lax.optimization_barrier((held, heads))
     chosen = call(take_kernel, shape(held.shape, BF16), [SM, HB], [sem], matching, held)
     partner = exchange(chosen)
     keep, give, rel_total = call(
-        own_kernel, (own_shape, own_shape, rel_shape), [SM] + [VM] * 3,
-        [mem(width, rows, F32), two_marks, rel_marks, neg, rel_wide],
-        group_counts, slab, relations, packed, flops=40 * unit,
+        own_kernel, (own_shape, own_shape, rel_shape), [SM] + [VM] * 2 + [HB] * 3,
+        [mem(width, rows, F32), two_marks, rel_marks, neg, two_wide, two_wide, two_wide, sems(3)],
+        group_counts, slab, packed, *own_rows, flops=32 * unit,
     )
     got = lax.ppermute(give, "edge", swap)
     other, pos_grads, right, tails, negs = call(
@@ -525,34 +587,40 @@
     rel_flat = shape((REL_RING * REL_WINDOW, LANES))
     saved = (weights, pos_grads, right, rel_rows, tails, negs)
     own, rel_keep, rel_give = call(
-        left_kernel, (own_shape, rel_flat, rel_flat), [SM] + [VM] * 5 + [HB] * 4 + [VM] * 3,
+        left_kernel, (own_shape, rel_flat, rel_flat), [SM] + [VM] * 5 + [HB] * 5 + [VM],
         [mem(width, padded, F32), one_mark, rel_marks, two_wide, two_wide, two_neg, two_wide, sems(4)],
-        group_counts, *idx, *saved, heads, keep, got, rel_total, flops=20 * unit,
+        group_counts, *idx, *saved, heads, got, rel_total, flops=20 * unit,
     )
     rel_got = lax.ppermute(rel_give, "dom", cores)
     grad_chosen = call(put_kernel, shape(grad_held.shape), [SM, VM], [sem], matching, grad_held, out_specs=HB)
     rel_keep, _ = lax.optimization_barrier((rel_keep, grad_chosen))
     rel_pieces = call(pair_kernel, shape((REL_RING, REL_WINDOW, LANES)), [VM, VM], [], rel_keep, rel_got)
     rel_held = exchange(rel_pieces, rings)
+    own, rel_pieces = lax.optimization_barrier((own, rel_pieces))
+    own = call(
+        rest_kernel, own_shape, [SM] + [VM] * 5 + [HB] * 3 + [VM] * 3, [one_mark, two_wide, two_wide, two_neg, sems(3)],
+        group_counts, *idx, *saved, own, keep, got, flops=15 * unit,
+    )
+    rel_held, grad_chosen, own = lax.optimization_barrier((rel_held, grad_chosen, own))
+    grad_pieces = exchange(grad_chosen)
     rel_sum = call(sum_kernel, shape((REL_WINDOW, LANES)), [VM], [], rel_held)
-    rel_held, grad_chosen = lax.optimization_barrier((rel_held, grad_chosen))
-    grad_pieces = exchange(grad_chosen)
     rel_sums = [rel_sum, lax.ppermute(rel_sum, "dom", planes), lax.ppermute(rel_sum, "edge", swap)]
     rel_sums += [lax.ppermute(rel_sum, ("dom", "edge"), corners)]
-    own, _ = lax.optimization_barrier((own, rel_sum))
-    own = call(
-        rest_kernel, own_shape, [SM] + [VM] * 5 + [HB] * 3 + [VM], [one_mark, two_wide, two_wide, two_neg, sems(3)],
-        group_counts, *idx, *saved, own, flops=15 * unit,
-    )
     own, grad_pieces, rel_sums = lax.optimization_barrier((own, grad_pieces, rel_sums))
-    half = call(add_kernel, own_shape, [VM] * 2, [], own, grad_pieces)
-    far = lax.ppermute(half, "edge", swap)
-    rel_sums, half = lax.optimization_barrier((rel_sums, half))
+    cut = 3 * width // 32 * 8
+    half_shapes = (shape((cut, middle)), shape((width - cut, middle)))
+    first, second = call(add_kernel, half_shapes, [VM] * 2, [], own, grad_pieces)
+    far = [lax.ppermute(x, "edge", swap) for x in (first, second)]
+    rel_sums, first = lax.optimization_barrier((rel_sums, first))
     rel_full = call(spread_kernel, shape(rel_pieces.shape), [VM] * 4, [], *rel_sums)
     rel_mine = exchange(rel_full, rings).reshape(rel_flat.shape)
+    rel_mine, far[0] = lax.optimization_barrier((rel_mine, far[0]))
     rel_far = lax.ppermute(rel_mine, "dom", cores)
     relation_grad = call(close_kernel, shape((width, rels)), [VM, VM], [], rel_mine, rel_far)
-    total = call(join_kernel, shape((width, rows)), [VM, VM], [], half, far)
+    whole = shape((width, rows))
+    total = call(join_kernel, whole, [VM] * 3, [sems(3)], first, second, far[0], out_specs=HB)
+    far[1], relation_grad = lax.optimization_barrier((far[1], relation_grad))
+    total = call(last_kernel, whole, [HB, VM], [sems(1)], total, far[1], out_specs=HB, aliases={0: 0})
     return total.T, relation_grad.T
 
 

time: 286 us -> 267 us (0.934)
  waiting for transfers between devices: 71 us -> 52.3 us
  local copies, waits for them, and re-layouts: 8.85 us -> 1.41 us
  Pallas kernels: 117 us -> 121 us
    ppermute x1 -> x2, waiting for transfers between devices: 17.8 us -> 6 us  [body(): far = [lax.ppermute(x, 'edge', swap) for x in (first, second)]]
    all_to_all x5, waiting for transfers between devices: 35.2 us -> 25.1 us  [exchange(): lax.all_to_all(x, 'dom', split_axis=0, concat_axis=0, tiled=True, axis_in...]
    unnamed x28 -> x14, local copies, waits for them, and re-layouts: 8.85 us -> 1.41 us
    pallas_call x14 -> x15, Pallas kernels: 117 us -> 121 us  [call(): pl.pallas_call(kernel, out_shape=outs, in_specs=specs, out_specs=jax.tree...]
    ppermute x1 -> x2, starting transfers between devices: 1.61 us -> 5.1 us  [body(): far = [lax.ppermute(x, 'edge', swap) for x in (first, second)]]
    ppermute x1, waiting for transfers between devices: 15 us -> 18.1 us  [body(): lax.ppermute(rel_sum, 'edge', swap)]
  transfers between devices with their start and end apart: 13 -> 14, of which waited for: 6 -> 8; matrix products, arithmetic and copies ran while one was open for 0% -> 0% of each run, Pallas kernels for 36% -> 42%
where the time goes in v3:
time: 267 us; the launch traced here: 264 us
  Pallas kernels  121 us (45%)
  starting transfers between devices  64.7 us (24%)
  waiting for transfers between devices  52.3 us (20%)
  blocking collectives  22.9 us (9%)
    pallas_call x15, Pallas kernels, call(): pl.pallas_call(kernel, out_shape=outs, in_specs=specs, out_specs=jax.tree...  121 us
    all_to_all x5, starting transfers between devices, exchange(): lax.all_to_all(x, 'dom', split_axis=0, concat_axis=0, tiled=True, axis_in...  49.7 us
    all_to_all x5, waiting for transfers between devices, exchange(): lax.all_to_all(x, 'dom', split_axis=0, concat_axis=0, tiled=True, axis_in...  25.1 us
    all_to_all x1, blocking collectives, exchange(): lax.all_to_all(x, 'dom', split_axis=0, concat_axis=0, tiled=True, axis_in...  22.9 us
    ppermute x1, waiting for transfers between devices, body(): lax.ppermute(rel_sum, 'edge', swap)  18.1 us
    ppermute x2, waiting for transfers between devices, body(): far = [lax.ppermute(x, 'edge', swap) for x in (first, second)]  6 us
  transfers between devices with their start and end apart: 14, of which 8 were waited for; matrix products, arithmetic and copies ran while one was open for 0% of the time, Pallas kernels for 42%

profile of v3, /device:TPU:1, one launch (start us, length us, event | category | flops | bytes accessed | tf_op | source)
XLA Modules:
  0.0 264.1 jit_solution(16326702108487354476)
XLA Ops:
  1.4 4.5 %collective-permute-start = (s32[3,2,2560]{2,1,0:T(2,128)S(1)}, s32[3,2,2560]{2,1,0:T(2,128)S(1)}, u32[]{:S(2)}, u32[]{:S(2)}) collective-permute-start(s32[3,2,2560]{2,1,0:T(2,128)S(1)} %pad_add_fusion.idx), channel_id=1, source_target_pairs={{0,1},{1,0},{2,3},{3,2},{4,5},{5,4},{6,7},{7,6},{8,9},{9,8},{10,11... | collective-permute-start | bytes 184328 | tf_op jit(solution)/shard_map/ppermute | solution.py:534
  5.9 3.0 %shard_map.95 = bf16[64,112,128]{2,1,0:T(8,128)(2,1)} custom-call(bf16[400,2048]{1,0:T(8,128)(2,1)} %bitcast.19), custom_call_target="tpu_custom_call" | custom-call | tf_op jit(solution)/shard_map/pallas_call | solution.py:497
  9.5 9.1 %all-to-all-start = ((bf16[64,112,128]{2,1,0:T(8,128)(2,1)}), bf16[64,112,128]{2,1,0:T(8,128)(2,1)}, u32[]{:S(2)}, u32[]{:S(2)}) async-start(bf16[64,112,128]{2,1,0:T(8,128)(2,1)} %shard_map.95), calls=%async_computation | async-start | bytes 3670016 | tf_op jit(solution)/shard_map/all_to_all | solution.py:529
  18.6 18.1 %shard_map.96 = (bf16[6,400,512]{2,1,0:T(8,128)(2,1)}, bf16[6,400,512]{2,1,0:T(8,128)(2,1)}, f32[6,1,2048]{2,1,0:T(1,128)}, bf16[3,400,512]{2,1,0:T(8,128)(2,1)}...) custom-call(s32[1,2]{1,0:T(1,128)} %counts.9, bf16[400,2048]{1,0:T(8,128)(2,1)} %bitcast.20, ...), custom_call_target="tpu_custom_call" | custom-call | flops 18454937600 | tf_op jit(solution)/shard_map/pallas_call | solution.py:497
  36.7 7.4 %all-to-all-done.held = bf16[64,112,128]{2,1,0:T(8,128)(2,1)} async-done(((bf16[64,112,128]{2,1,0:T(8,128)(2,1)}), bf16[64,112,128]{2,1,0:T(8,128)(2,1)}, u32[]{:S(2)}, u32[]{:S(2)}) %all-to-all-start) | async-done | bytes 1835040 | tf_op jit(solution)/shard_map/all_to_all | solution.py:529
  44.1 3.4 %shard_map.97 = bf16[64,112,128]{2,1,0:T(8,128)(2,1)} custom-call(s32[64]{0:T(128)} %matching.3, bf16[64,112,128]{2,1,0:T(8,128)(2,1)} %all-to-all-done.held), custom_call_target="tpu_custom_call" | custom-call | tf_op jit(solution)/shard_map/pallas_call | solution.py:497
  47.5 5.8 %all-to-all-start.1 = ((bf16[64,112,128]{2,1,0:T(8,128)(2,1)}), bf16[64,112,128]{2,1,0:T(8,128)(2,1)}, u32[]{:S(2)}, u32[]{:S(2)}) async-start(bf16[64,112,128]{2,1,0:T(8,128)(2,1)} %shard_map.97), calls=%async_computation.1 | async-start | bytes 3670016 | tf_op jit(solution)/shard_map/all_to_all | solution.py:529
  53.2 32.6 %shard_map.99 = (f32[400,1024]{1,0:T(8,128)}, f32[400,1024]{1,0:T(8,128)}, f32[400,1408]{1,0:T(8,128)}) custom-call(s32[1,2]{1,0:T(1,128)} %counts.9, bf16[400,2048]{1,0:T(8,128)(2,1)} %bitcast.21, s32[3,2,2560]{2,1,0:T(2,128)} %copy-done.5, bf16[3,400,512]{2,1,0:T(8,128)(2,1)} %get-tuple-element.58.heads, bf16[3,400,512]{2,1,0:T(8,128)(2,1)} %get-tuple-element.59.rels, ...), custom_call_target="tpu_custom_call" | custom-call | flops 26843545600 | tf_op jit(solution)/shard_map/pallas_call | solution.py:497
  85.9 18.5 %shard_map.98 = (f32[64,56,128]{2,1,0:T(8,128)}, f32[6,1,512]{2,1,0:T(1,128)}, bf16[400,2048]{1,0:T(8,128)(2,1)}, bf16[6,400,512]{2,1,0:T(8,128)(2,1)}, bf16[6,2048,512]{2,1,0:T(8,128)(2,1)}) custom-call(s32[1,2]{1,0:T(1,128)} %counts.9, bf16[64,112,128]{2,1,0:T(8,128)(2,1)} %all-to-all-done.1.pieces, s32[3,2,2560]{2,1,0:T(2,128)} %copy-done.5, ...), custom_call_target="tpu_custom_call" | custom-call | flops 25165824000 | tf_op jit(solution)/shard_map/pallas_call | solution.py:497
  104.4 22.0 %all-to-all-start.2 = ((f32[64,56,128]{2,1,0:T(8,128)}), f32[64,56,128]{2,1,0:T(8,128)}, u32[]{:S(2)}, u32[]{:S(2)}) async-start(f32[64,56,128]{2,1,0:T(8,128)} %get-tuple-element.64), calls=%async_computation.2 | async-start | bytes 3670016 | tf_op jit(solution)/shard_map/all_to_all | solution.py:529
  126.5 19.6 %shard_map.100 = (f32[400,1024]{1,0:T(8,128)}, f32[2304,128]{1,0:T(8,128)}, f32[2304,128]{1,0:T(8,128)}) custom-call(s32[1,2]{1,0:T(1,128)} %counts.9, s32[3,2,2560]{2,1,0:T(2,128)} %copy-done.5, s32[3,2,2560]{2,1,0:T(2,128)} %copy-done.6, f32[6,1,2048]{2,1,0:T(1,128)} %get-tuple-element.48.weights, f32[6,1,512]{2,1,0:T(1,128)} %get-tuple-element.54.pos_grads, ...), custom_call_target="tpu_custom_call" | custom-call | flops 16777216000 | tf_op jit(solution)/shard_map/pallas_call | solution.py:497
  146.6 5.3 %all-to-all-done.2.held = f32[64,56,128]{2,1,0:T(8,128)} async-done(((f32[64,56,128]{2,1,0:T(8,128)}), f32[64,56,128]{2,1,0:T(8,128)}, u32[]{:S(2)}, u32[]{:S(2)}) %all-to-all-start.2) | async-done | bytes 1835040 | tf_op jit(solution)/shard_map/all_to_all | solution.py:529
  154.7 2.8 %shard_map.102 = f32[16,144,128]{2,1,0:T(8,128)} custom-call(f32[2304,128]{1,0:T(8,128)} %get-tuple-element.65.keep, f32[2304,128]{1,0:T(8,128)} %collective-permute-done.2.got), custom_call_target="tpu_custom_call" | custom-call | tf_op jit(solution)/shard_map/pallas_call | solution.py:497
  157.5 4.4 %all-to-all-start.3 = ((f32[16,144,128]{2,1,0:T(8,128)}), f32[16,144,128]{2,1,0:T(8,128)}, u32[]{:S(2)}, u32[]{:S(2)}) async-start(f32[16,144,128]{2,1,0:T(8,128)} %shard_map.102), calls=%async_computation.3 | async-start | bytes 2359296 | tf_op jit(solution)/shard_map/all_to_all | solution.py:529
  161.9 4.7 %shard_map.103.own = f32[400,1024]{1,0:T(8,128)} custom-call(s32[1,2]{1,0:T(1,128)} %counts.9, s32[3,2,2560]{2,1,0:T(2,128)} %copy-done.5, s32[3,2,2560]{2,1,0:T(2,128)} %copy-done.6, f32[6,1,2048]{2,1,0:T(1,128)} %get-tuple-element.48.weights, f32[6,1,512]{2,1,0:T(1,128)} %get-tuple-element.54.pos_grads, bf16[400,2048]{1,0:T(8,128)(2,1)} %get-tuple-element.55.right, ...), custom_call_target="tpu_custom_call" | custom-call | flops 12582912000 | tf_op jit(solution)/shard_map/pallas_call | solution.py:497
  166.6 12.4 %all-to-all-done.3.held = f32[16,144,128]{2,1,0:T(8,128)} async-done(((f32[16,144,128]{2,1,0:T(8,128)}), f32[16,144,128]{2,1,0:T(8,128)}, u32[]{:S(2)}, u32[]{:S(2)}) %all-to-all-start.3) | async-done | bytes 1179680 | tf_op jit(solution)/shard_map/all_to_all | solution.py:529
  179.0 8.5 %all-to-all-start.4 = ((f32[64,56,128]{2,1,0:T(8,128)}), f32[64,56,128]{2,1,0:T(8,128)}, u32[]{:S(2)}, u32[]{:S(2)}) async-start(f32[64,56,128]{2,1,0:T(8,128)} %shard_map.101), calls=%async_computation.4 | async-start | bytes 3670016 | tf_op jit(solution)/shard_map/all_to_all | solution.py:529
  189.4 2.8 %collective-permute-start.5 = (f32[144,128]{1,0:T(8,128)}, f32[144,128]{1,0:T(8,128)S(1)}, u32[]{:S(2)}, u32[]{:S(2)}) collective-permute-start(f32[144,128]{1,0:T(8,128)} %shard_map.104.a), channel_id=1, source_target_pairs={{0,65},{1,64},{2,67},{3,66},{4,69},{5,68},{6,71},{7,70},{8,73},{9,... | collective-permute-start | bytes 221192 | tf_op jit(solution)/shard_map/ppermute | solution.py:608
  194.6 18.1 %collective-permute-done.4.c = f32[144,128]{1,0:T(8,128)S(1)} collective-permute-done((f32[144,128]{1,0:T(8,128)}, f32[144,128]{1,0:T(8,128)S(1)}, u32[]{:S(2)}, u32[]{:S(2)}) %collective-permute-start.4) | collective-permute-done | bytes 73760 | tf_op jit(solution)/shard_map/ppermute | solution.py:607
  213.9 3.4 %shard_map.105 = (f32[296,1024]{1,0:T(8,128)}, f32[104,1024]{1,0:T(8,128)}) custom-call(f32[400,1024]{1,0:T(8,128)} %shard_map.103.own, f32[64,56,128]{2,1,0:T(8,128)} %all-to-all-done.4.pieces), custom_call_target="tpu_custom_call" | custom-call | tf_op jit(solution)/shard_map/pallas_call | solution.py:497
  222.1 22.9 %all_to_all.30 = f32[16,144,128]{2,1,0:T(8,128)} all-to-all(f32[16,144,128]{2,1,0:T(8,128)} %shard_map.106), channel_id=1, replica_groups={{0,4,8,12,16,20,24,28,32,36,40,44,48,52,56,60},{2,6,10,14,18,22,26,30,3..., dimensions={0} | all-to-all | bytes 2359296 | tf_op jit(solution)/shard_map/all_to_all | solution.py:529
  250.9 3.4 %shard_map.107.begun = f32[400,2048]{1,0:T(8,128)} custom-call(f32[296,1024]{1,0:T(8,128)} %get-tuple-element.80.first, f32[104,1024]{1,0:T(8,128)} %get-tuple-element.81.second, f32[296,1024]{1,0:T(8,128)} %collective-permute-done.6.far), custom_call_target="tpu_custom_call" | custom-call | tf_op jit(solution)/shard_map/pallas_call | solution.py:497
  254.3 3.1 %shard_map.108 = f32[400,1345]{1,0:T(8,128)} custom-call(f32[2304,128]{1,0:T(8,128)} %bitcast.10.mine, f32[2304,128]{1,0:T(8,128)} %collective-permute-done.8.theirs), custom_call_target="tpu_custom_call" | custom-call | tf_op jit(solution)/shard_map/pallas_call | solution.py:497
  257.5 3.9 %collective-permute-done.7.far = f32[104,1024]{1,0:T(8,128)S(1)} collective-permute-done((f32[104,1024]{1,0:T(8,128)S(1)}, f32[104,1024]{1,0:T(8,128)S(1)}, u32[]{:S(2)}, u32[]{:S(2)}) %collective-permute-start.7) | collective-permute-done | bytes 426016 | tf_op jit(solution)/shard_map/ppermute | solution.py:613
  (35 shorter events, 23.5 us)
Async XLA Ops:
  1.4 7.5 %copy-start.5 = (s32[3,2,2560]{2,1,0:T(2,128)}, s32[3,2,2560]{2,1,0:T(2,128)S(1)}, u32[]{:S(2)}) copy-start(s32[3,2,2560]{2,1,0:T(2,128)S(1)} %pad_add_fusion.idx) | copy-start | bytes 184324
  1.4 7.5 %collective-permute-start = (s32[3,2,2560]{2,1,0:T(2,128)S(1)}, s32[3,2,2560]{2,1,0:T(2,128)S(1)}, u32[]{:S(2)}, u32[]{:S(2)}) collective-permute-start(s32[3,2,2560]{2,1,0:T(2,128)S(1)} %pad_add_fusion.idx), channel_id=1, source_target_pairs={{0,1},{1,0},{2,3},{3,2},{4,5},{5,4},{6,7},{7,6},{8,9},{9,8},{10,11... | collective-permute-start | bytes 184328 | tf_op jit(solution)/shard_map/ppermute | solution.py:534
  8.9 0.6 copy-start.6
  9.5 34.6 %all-to-all-start = ((bf16[64,112,128]{2,1,0:T(8,128)(2,1)}), bf16[64,112,128]{2,1,0:T(8,128)(2,1)}, u32[]{:S(2)}, u32[]{:S(2)}) async-start(bf16[64,112,128]{2,1,0:T(8,128)(2,1)} %shard_map.95), calls=%async_computation | async-start | bytes 3670016 | tf_op jit(solution)/shard_map/all_to_all | solution.py:529
  47.5 38.5 %all-to-all-start.1 = ((bf16[64,112,128]{2,1,0:T(8,128)(2,1)}), bf16[64,112,128]{2,1,0:T(8,128)(2,1)}, u32[]{:S(2)}, u32[]{:S(2)}) async-start(bf16[64,112,128]{2,1,0:T(8,128)(2,1)} %shard_map.97), calls=%async_computation.1 | async-start | bytes 3670016 | tf_op jit(solution)/shard_map/all_to_all | solution.py:529
  85.8 40.6 %collective-permute-start.1 = (f32[400,1024]{1,0:T(8,128)}, f32[400,1024]{1,0:T(8,128)}, u32[]{:S(2)}, u32[]{:S(2)}) collective-permute-start(f32[400,1024]{1,0:T(8,128)} %get-tuple-element.61), channel_id=1, source_target_pairs={{0,1},{1,0},{2,3},{3,2},{4,5},{5,4},{6,7},{7,6},{8,9},{9,8},{10,11... | collective-permute-start | bytes 4915208 | tf_op jit(solution)/shard_map/ppermute | solution.py:571
  104.4 47.6 %all-to-all-start.2 = ((f32[64,56,128]{2,1,0:T(8,128)}), f32[64,56,128]{2,1,0:T(8,128)}, u32[]{:S(2)}, u32[]{:S(2)}) async-start(f32[64,56,128]{2,1,0:T(8,128)} %get-tuple-element.64), calls=%async_computation.2 | async-start | bytes 3670016 | tf_op jit(solution)/shard_map/all_to_all | solution.py:529
  146.0 8.7 %collective-permute-start.2 = (f32[2304,128]{1,0:T(8,128)}, f32[2304,128]{1,0:T(8,128)}, u32[]{:S(2)}, u32[]{:S(2)}) collective-permute-start(f32[2304,128]{1,0:T(8,128)} %get-tuple-element.66), channel_id=1, source_target_pairs={{0,2},{2,0},{4,6},{6,4},{8,10},{10,8},{12,14},{14,12},{16,18},{18,... | collective-permute-start | bytes 3538952 | tf_op jit(solution)/shard_map/ppermute | solution.py:594
  157.5 21.5 %all-to-all-start.3 = ((f32[16,144,128]{2,1,0:T(8,128)}), f32[16,144,128]{2,1,0:T(8,128)}, u32[]{:S(2)}, u32[]{:S(2)}) async-start(f32[16,144,128]{2,1,0:T(8,128)} %shard_map.102), calls=%async_computation.3 | async-start | bytes 2359296 | tf_op jit(solution)/shard_map/all_to_all | solution.py:529
  179.0 34.9 %all-to-all-start.4 = ((f32[64,56,128]{2,1,0:T(8,128)}), f32[64,56,128]{2,1,0:T(8,128)}, u32[]{:S(2)}, u32[]{:S(2)}) async-start(f32[64,56,128]{2,1,0:T(8,128)} %shard_map.101), calls=%async_computation.4 | async-start | bytes 3670016 | tf_op jit(solution)/shard_map/all_to_all | solution.py:529
  189.4 5.2 %collective-permute-start.5 = (f32[144,128]{1,0:T(8,128)}, f32[144,128]{1,0:T(8,128)S(1)}, u32[]{:S(2)}, u32[]{:S(2)}) collective-permute-start(f32[144,128]{1,0:T(8,128)} %shard_map.104.a), channel_id=1, source_target_pairs={{0,65},{1,64},{2,67},{3,66},{4,69},{5,68},{6,71},{7,70},{8,73},{9,... | collective-permute-start | bytes 221192 | tf_op jit(solution)/shard_map/ppermute | solution.py:608
  192.3 20.4 %collective-permute-start.4 = (f32[144,128]{1,0:T(8,128)}, f32[144,128]{1,0:T(8,128)S(1)}, u32[]{:S(2)}, u32[]{:S(2)}) collective-permute-start(f32[144,128]{1,0:T(8,128)} %shard_map.104.a), channel_id=1, source_target_pairs={{0,1},{1,0},{2,3},{3,2},{4,5},{5,4},{6,7},{7,6},{8,9},{9,8},{10,11... | collective-permute-start | bytes 221192 | tf_op jit(solution)/shard_map/ppermute | solution.py:607
  192.7 21.2 %collective-permute-start.3 = (f32[144,128]{1,0:T(8,128)}, f32[144,128]{1,0:T(8,128)S(1)}, u32[]{:S(2)}, u32[]{:S(2)}) collective-permute-start(f32[144,128]{1,0:T(8,128)} %shard_map.104.a), channel_id=1, source_target_pairs={{0,64},{2,66},{4,68},{6,70},{8,72},{10,74},{12,76},{14,78},{16,80}... | collective-permute-start | bytes 221192 | tf_op jit(solution)/shard_map/ppermute | solution.py:607
  194.6 22.8 %copy-start.2 = (f32[144,128]{1,0:T(8,128)}, f32[144,128]{1,0:T(8,128)S(1)}, u32[]{:S(2)}) copy-start(f32[144,128]{1,0:T(8,128)S(1)} %collective-permute-done.5.d) | copy-start | bytes 221188
  212.7 4.7 %copy-start.3 = (f32[144,128]{1,0:T(8,128)}, f32[144,128]{1,0:T(8,128)S(1)}, u32[]{:S(2)}) copy-start(f32[144,128]{1,0:T(8,128)S(1)} %collective-permute-done.4.c) | copy-start | bytes 221188
  213.9 3.5 %copy-start.4 = (f32[144,128]{1,0:T(8,128)}, f32[144,128]{1,0:T(8,128)S(1)}, u32[]{:S(2)}) copy-start(f32[144,128]{1,0:T(8,128)S(1)} %collective-permute-done.3.b) | copy-start | bytes 221188
  217.4 31.0 %copy-start = (f32[104,1024]{1,0:T(8,128)S(1)}, f32[104,1024]{1,0:T(8,128)}, u32[]{:S(2)}) copy-start(f32[104,1024]{1,0:T(8,128)} %get-tuple-element.81.second) | copy-start | bytes 1277956
  217.4 29.6 %collective-permute-start.6 = (f32[296,1024]{1,0:T(8,128)}, f32[296,1024]{1,0:T(8,128)}, u32[]{:S(2)}, u32[]{:S(2)}) collective-permute-start(f32[296,1024]{1,0:T(8,128)} %get-tuple-element.80.first), channel_id=1, source_target_pairs={{0,1},{1,0},{2,3},{3,2},{4,5},{5,4},{6,7},{7,6},{8,9},{9,8},{10,11... | collective-permute-start | bytes 3637256 | tf_op jit(solution)/shard_map/ppermute | solution.py:613
  247.1 7.3 %collective-permute-start.8 = (f32[2304,128]{1,0:T(8,128)}, f32[2304,128]{1,0:T(8,128)}, u32[]{:S(2)}, u32[]{:S(2)}) collective-permute-start(f32[2304,128]{1,0:T(8,128)} %bitcast.10.mine), channel_id=1, source_target_pairs={{0,2},{2,0},{4,6},{6,4},{8,10},{10,8},{12,14},{14,12},{16,18},{18,... | collective-permute-start | bytes 3538952 | tf_op jit(solution)/shard_map/ppermute | solution.py:618
  248.4 13.0 %collective-permute-start.7 = (f32[104,1024]{1,0:T(8,128)S(1)}, f32[104,1024]{1,0:T(8,128)S(1)}, u32[]{:S(2)}, u32[]{:S(2)}) collective-permute-start(f32[104,1024]{1,0:T(8,128)S(1)} %copy-done), channel_id=1, source_target_pairs={{0,1},{1,0},{2,3},{3,2},{4,5},{5,4},{6,7},{7,6},{8,9},{9,8},{10,11... | collective-permute-start | bytes 1277960 | tf_op jit(solution)/shard_map/ppermute | solution.py:613
  261.4 0.8 copy-start.1

commit v4 on v3

--- a/solution.py
+++ b/solution.py
@@ -18,6 +18,7 @@
 SLAB_STARTS = (0, 96, 192, 288)
 GRAD_WINDOW = 56
 GRAD_STARTS = (0, 56, 112, 168, 224, 280, 336, 344)
+EARLY_ROWS = 168
 REL_WINDOW = 144
 REL_RING = 16
 
@@ -593,34 +594,36 @@
     )
     rel_got = lax.ppermute(rel_give, "dom", cores)
     grad_chosen = call(put_kernel, shape(grad_held.shape), [SM, VM], [sem], matching, grad_held, out_specs=HB)
-    rel_keep, _ = lax.optimization_barrier((rel_keep, grad_chosen))
+    grad_pieces = exchange(grad_chosen)
+    rel_keep, own, grad_chosen = lax.optimization_barrier((rel_keep, own, grad_chosen))
     rel_pieces = call(pair_kernel, shape((REL_RING, REL_WINDOW, LANES)), [VM, VM], [], rel_keep, rel_got)
-    rel_held = exchange(rel_pieces, rings)
-    own, rel_pieces = lax.optimization_barrier((own, rel_pieces))
     own = call(
         rest_kernel, own_shape, [SM] + [VM] * 5 + [HB] * 3 + [VM] * 3, [one_mark, two_wide, two_wide, two_neg, sems(3)],
         group_counts, *idx, *saved, own, keep, got, flops=15 * unit,
     )
-    rel_held, grad_chosen, own = lax.optimization_barrier((rel_held, grad_chosen, own))
-    grad_pieces = exchange(grad_chosen)
+    own, grad_pieces, rel_pieces = lax.optimization_barrier((own, grad_pieces, rel_pieces))
+    cut = EARLY_ROWS
+    half_shapes = (shape((cut, middle)), shape((width - cut, middle)))
+    first, second = call(add_kernel, half_shapes, [VM] * 2, [], own, grad_pieces)
+    far = [lax.ppermute(first, "edge", swap), None]
+    rel_pieces, second = lax.optimization_barrier((rel_pieces, second))
+    rel_held = exchange(rel_pieces, rings)
+    whole = shape((width, rows))
+    total = call(join_kernel, whole, [VM] * 3, [sems(3)], first, second, far[0], out_specs=HB, flops=60 * unit)
+    rel_held, total = lax.optimization_barrier((rel_held, total))
     rel_sum = call(sum_kernel, shape((REL_WINDOW, LANES)), [VM], [], rel_held)
     rel_sums = [rel_sum, lax.ppermute(rel_sum, "dom", planes), lax.ppermute(rel_sum, "edge", swap)]
     rel_sums += [lax.ppermute(rel_sum, ("dom", "edge"), corners)]
-    own, grad_pieces, rel_sums = lax.optimization_barrier((own, grad_pieces, rel_sums))
-    cut = 3 * width // 32 * 8
-    half_shapes = (shape((cut, middle)), shape((width - cut, middle)))
-    first, second = call(add_kernel, half_shapes, [VM] * 2, [], own, grad_pieces)
-    far = [lax.ppermute(x, "edge", swap) for x in (first, second)]
-    rel_sums, first = lax.optimization_barrier((rel_sums, first))
+    second, rel_sums = lax.optimization_barrier((second, rel_sums))
+    far[1] = lax.ppermute(second, "edge", swap)
     rel_full = call(spread_kernel, shape(rel_pieces.shape), [VM] * 4, [], *rel_sums)
     rel_mine = exchange(rel_full, rings).reshape(rel_flat.shape)
-    rel_mine, far[0] = lax.optimization_barrier((rel_mine, far[0]))
+    total = call(
+        last_kernel, whole, [HB, VM], [sems(1)], total, far[1], out_specs=HB, aliases={0: 0}, flops=60 * unit
+    )
+    rel_mine, total = lax.optimization_barrier((rel_mine, total))
     rel_far = lax.ppermute(rel_mine, "dom", cores)
     relation_grad = call(close_kernel, shape((width, rels)), [VM, VM], [], rel_mine, rel_far)
-    whole = shape((width, rows))
-    total = call(join_kernel, whole, [VM] * 3, [sems(3)], first, second, far[0], out_specs=HB)
-    far[1], relation_grad = lax.optimization_barrier((far[1], relation_grad))
-    total = call(last_kernel, whole, [HB, VM], [sems(1)], total, far[1], out_specs=HB, aliases={0: 0})
     return total.T, relation_grad.T
 
 

time: 267 us -> 260 us (0.974)
  Pallas kernels: 121 us -> 150 us
  blocking collectives: 22.9 us -> 0 us
  starting transfers between devices: 64.7 us -> 57.3 us
  waiting for transfers between devices: 52.3 us -> 48.3 us
    pallas_call x15, Pallas kernels: 121 us -> 150 us  [call(): pl.pallas_call(kernel, out_shape=outs, in_specs=specs, out_specs=jax.tree...]
    all_to_all x1 -> x0, blocking collectives: 22.9 us -> none  [exchange(): lax.all_to_all(x, 'dom', split_axis=0, concat_axis=0, tiled=True, axis_in...]
    ppermute x2, waiting for transfers between devices: 6 us -> 25.2 us  [the longest x1 12.7 us: body(): far[1] = lax.ppermute(second, 'edge', swap)]
    ppermute x1, waiting for transfers between devices: 18.1 us -> 2.48 us  [body(): lax.ppermute(rel_sum, 'edge', swap)]
    all_to_all x5 -> x6, waiting for transfers between devices: 25.1 us -> 16.2 us  [exchange(): lax.all_to_all(x, 'dom', split_axis=0, concat_axis=0, tiled=True, axis_in...]
    all_to_all x5 -> x6, starting transfers between devices: 49.7 us -> 41.2 us  [exchange(): lax.all_to_all(x, 'dom', split_axis=0, concat_axis=0, tiled=True, axis_in...]
    ppermute x1, starting transfers between devices: 1.34 us -> 5.12 us  [body(): rel_far = lax.ppermute(rel_mine, 'dom', cores)]
    ppermute x1, waiting for transfers between devices: 0.01 us -> 2.82 us  [body(): rel_far = lax.ppermute(rel_mine, 'dom', cores)]
  transfers between devices with their start and end apart: 14 -> 15, of which waited for: 8 -> 9; matrix products, arithmetic and copies ran while one was open for 0% -> 0% of each run, Pallas kernels for 42% -> 53%
where the time goes in v4:
time: 260 us; the launch traced here: 259 us
  Pallas kernels  150 us (58%)
  starting transfers between devices  57.3 us (22%)
  waiting for transfers between devices  48.3 us (19%)
    pallas_call x15, Pallas kernels, call(): pl.pallas_call(kernel, out_shape=outs, in_specs=specs, out_specs=jax.tree...  150 us
    all_to_all x6, starting transfers between devices, exchange(): lax.all_to_all(x, 'dom', split_axis=0, concat_axis=0, tiled=True, axis_in...  41.2 us
    all_to_all x6, waiting for transfers between devices, exchange(): lax.all_to_all(x, 'dom', split_axis=0, concat_axis=0, tiled=True, axis_in...  16.2 us
    ppermute x1, waiting for transfers between devices, body(): far[1] = lax.ppermute(second, 'edge', swap)  12.7 us
    ppermute x1, waiting for transfers between devices, body(): far = [lax.ppermute(first, 'edge', swap), None]  12.5 us
  transfers between devices with their start and end apart: 15, of which 9 were waited for; matrix products, arithmetic and copies ran while one was open for 0% of the time, Pallas kernels for 53%

profile of v4, /device:TPU:1, one launch (start us, length us, event | category | flops | bytes accessed | tf_op | source)
XLA Modules:
  0.0 258.9 jit_solution(4727042557626332863)
XLA Ops:
  1.4 4.5 %collective-permute-start = (s32[3,2,2560]{2,1,0:T(2,128)S(1)}, s32[3,2,2560]{2,1,0:T(2,128)S(1)}, u32[]{:S(2)}, u32[]{:S(2)}) collective-permute-start(s32[3,2,2560]{2,1,0:T(2,128)S(1)} %pad_add_fusion.idx), channel_id=1, source_target_pairs={{0,1},{1,0},{2,3},{3,2},{4,5},{5,4},{6,7},{7,6},{8,9},{9,8},{10,11... | collective-permute-start | bytes 184328 | tf_op jit(solution)/shard_map/ppermute | solution.py:535
  5.9 3.0 %shard_map.95 = bf16[64,112,128]{2,1,0:T(8,128)(2,1)} custom-call(bf16[400,2048]{1,0:T(8,128)(2,1)} %bitcast.18), custom_call_target="tpu_custom_call" | custom-call | tf_op jit(solution)/shard_map/pallas_call | solution.py:498
  9.5 9.1 %all-to-all-start = ((bf16[64,112,128]{2,1,0:T(8,128)(2,1)}), bf16[64,112,128]{2,1,0:T(8,128)(2,1)}, u32[]{:S(2)}, u32[]{:S(2)}) async-start(bf16[64,112,128]{2,1,0:T(8,128)(2,1)} %shard_map.95), calls=%async_computation | async-start | bytes 3670016 | tf_op jit(solution)/shard_map/all_to_all | solution.py:530
  18.6 23.3 %shard_map.96 = (bf16[6,400,512]{2,1,0:T(8,128)(2,1)}, bf16[6,400,512]{2,1,0:T(8,128)(2,1)}, f32[6,1,2048]{2,1,0:T(1,128)}, bf16[3,400,512]{2,1,0:T(8,128)(2,1)}...) custom-call(s32[1,2]{1,0:T(1,128)} %counts.9, bf16[400,2048]{1,0:T(8,128)(2,1)} %bitcast.19, ...), custom_call_target="tpu_custom_call" | custom-call | flops 18454937600 | tf_op jit(solution)/shard_map/pallas_call | solution.py:498
  44.1 3.4 %shard_map.97 = bf16[64,112,128]{2,1,0:T(8,128)(2,1)} custom-call(s32[64]{0:T(128)} %matching.3, bf16[64,112,128]{2,1,0:T(8,128)(2,1)} %all-to-all-done.held), custom_call_target="tpu_custom_call" | custom-call | tf_op jit(solution)/shard_map/pallas_call | solution.py:498
  47.5 6.6 %all-to-all-start.1 = ((bf16[64,112,128]{2,1,0:T(8,128)(2,1)}), bf16[64,112,128]{2,1,0:T(8,128)(2,1)}, u32[]{:S(2)}, u32[]{:S(2)}) async-start(bf16[64,112,128]{2,1,0:T(8,128)(2,1)} %shard_map.97), calls=%async_computation.1 | async-start | bytes 3670016 | tf_op jit(solution)/shard_map/all_to_all | solution.py:530
  54.1 32.6 %shard_map.99 = (f32[400,1024]{1,0:T(8,128)}, f32[400,1024]{1,0:T(8,128)}, f32[400,1408]{1,0:T(8,128)}) custom-call(s32[1,2]{1,0:T(1,128)} %counts.9, bf16[400,2048]{1,0:T(8,128)(2,1)} %bitcast.20, s32[3,2,2560]{2,1,0:T(2,128)} %copy-done.3, bf16[3,400,512]{2,1,0:T(8,128)(2,1)} %get-tuple-element.54.heads, bf16[3,400,512]{2,1,0:T(8,128)(2,1)} %get-tuple-element.55.rels, ...), custom_call_target="tpu_custom_call" | custom-call | flops 26843545600 | tf_op jit(solution)/shard_map/pallas_call | solution.py:498
  86.8 31.8 %shard_map.98 = (f32[64,56,128]{2,1,0:T(8,128)}, f32[6,1,512]{2,1,0:T(1,128)}, bf16[400,2048]{1,0:T(8,128)(2,1)}, bf16[6,400,512]{2,1,0:T(8,128)(2,1)}, bf16[6,2048,512]{2,1,0:T(8,128)(2,1)}) custom-call(s32[1,2]{1,0:T(1,128)} %counts.9, bf16[64,112,128]{2,1,0:T(8,128)(2,1)} %all-to-all-done.1.pieces, s32[3,2,2560]{2,1,0:T(2,128)} %copy-done.3, ...), custom_call_target="tpu_custom_call" | custom-call | flops 25165824000 | tf_op jit(solution)/shard_map/pallas_call | solution.py:498
  118.6 11.3 %all-to-all-start.2 = ((f32[64,56,128]{2,1,0:T(8,128)}), f32[64,56,128]{2,1,0:T(8,128)}, u32[]{:S(2)}, u32[]{:S(2)}) async-start(f32[64,56,128]{2,1,0:T(8,128)} %get-tuple-element.61), calls=%async_computation.2 | async-start | bytes 3670016 | tf_op jit(solution)/shard_map/all_to_all | solution.py:530
  129.9 19.6 %shard_map.100 = (f32[400,1024]{1,0:T(8,128)}, f32[2304,128]{1,0:T(8,128)}, f32[2304,128]{1,0:T(8,128)}) custom-call(s32[1,2]{1,0:T(1,128)} %counts.9, s32[3,2,2560]{2,1,0:T(2,128)} %copy-done.3, s32[3,2,2560]{2,1,0:T(2,128)} %copy-done.5, f32[6,1,2048]{2,1,0:T(1,128)} %get-tuple-element.44.weights, f32[6,1,512]{2,1,0:T(1,128)} %get-tuple-element.50.pos_grads, ...), custom_call_target="tpu_custom_call" | custom-call | flops 16777216000 | tf_op jit(solution)/shard_map/pallas_call | solution.py:498
  149.6 5.9 %all-to-all-done.2.held = f32[64,56,128]{2,1,0:T(8,128)} async-done(((f32[64,56,128]{2,1,0:T(8,128)}), f32[64,56,128]{2,1,0:T(8,128)}, u32[]{:S(2)}, u32[]{:S(2)}) %all-to-all-start.2) | async-done | bytes 1835040 | tf_op jit(solution)/shard_map/all_to_all | solution.py:530
  158.1 5.5 %all-to-all-start.3 = ((f32[64,56,128]{2,1,0:T(8,128)}), f32[64,56,128]{2,1,0:T(8,128)}, u32[]{:S(2)}, u32[]{:S(2)}) async-start(f32[64,56,128]{2,1,0:T(8,128)} %shard_map.101), calls=%async_computation.3 | async-start | bytes 3670016 | tf_op jit(solution)/shard_map/all_to_all | solution.py:530
  163.6 2.8 %shard_map.103 = f32[16,144,128]{2,1,0:T(8,128)} custom-call(f32[2304,128]{1,0:T(8,128)} %get-tuple-element.64.keep, f32[2304,128]{1,0:T(8,128)} %collective-permute-done.2.got), custom_call_target="tpu_custom_call" | custom-call | tf_op jit(solution)/shard_map/pallas_call | solution.py:498
  166.4 15.3 %shard_map.102.own = f32[400,1024]{1,0:T(8,128)} custom-call(s32[1,2]{1,0:T(1,128)} %counts.9, s32[3,2,2560]{2,1,0:T(2,128)} %copy-done.3, s32[3,2,2560]{2,1,0:T(2,128)} %copy-done.5, f32[6,1,2048]{2,1,0:T(1,128)} %get-tuple-element.44.weights, f32[6,1,512]{2,1,0:T(1,128)} %get-tuple-element.50.pos_grads, bf16[400,2048]{1,0:T(8,128)(2,1)} %get-tuple-element.51.right, ...), custom_call_target="tpu_custom_call" | custom-call | flops 12582912000 | tf_op jit(solution)/shard_map/pallas_call | solution.py:498
  181.7 7.5 %all-to-all-done.3.pieces = f32[64,56,128]{2,1,0:T(8,128)} async-done(((f32[64,56,128]{2,1,0:T(8,128)}), f32[64,56,128]{2,1,0:T(8,128)}, u32[]{:S(2)}, u32[]{:S(2)}) %all-to-all-start.3) | async-done | bytes 1835040 | tf_op jit(solution)/shard_map/all_to_all | solution.py:530
  189.2 3.4 %shard_map.104 = (f32[168,1024]{1,0:T(8,128)}, f32[232,1024]{1,0:T(8,128)}) custom-call(f32[400,1024]{1,0:T(8,128)} %shard_map.102.own, f32[64,56,128]{2,1,0:T(8,128)} %all-to-all-done.3.pieces), custom_call_target="tpu_custom_call" | custom-call | tf_op jit(solution)/shard_map/pallas_call | solution.py:498
  194.0 4.4 %all-to-all-start.4 = ((f32[16,144,128]{2,1,0:T(8,128)}), f32[16,144,128]{2,1,0:T(8,128)}, u32[]{:S(2)}, u32[]{:S(2)}) async-start(f32[16,144,128]{2,1,0:T(8,128)} %shard_map.103), calls=%async_computation.4 | async-start | bytes 2359296 | tf_op jit(solution)/shard_map/all_to_all | solution.py:530
  198.4 12.5 %collective-permute-done.3.far = f32[168,1024]{1,0:T(8,128)S(1)} collective-permute-done((f32[168,1024]{1,0:T(8,128)}, f32[168,1024]{1,0:T(8,128)S(1)}, u32[]{:S(2)}, u32[]{:S(2)}) %collective-permute-start.3) | collective-permute-done | bytes 688160 | tf_op jit(solution)/shard_map/ppermute | solution.py:608
  211.7 3.0 %shard_map.105.begun = f32[400,2048]{1,0:T(8,128)} custom-call(f32[168,1024]{1,0:T(8,128)} %get-tuple-element.72.first, f32[232,1024]{1,0:T(8,128)} %get-tuple-element.79.second, f32[168,1024]{1,0:T(8,128)} %copy-done.4), custom_call_target="tpu_custom_call" | custom-call | flops 50331648000 | tf_op jit(solution)/shard_map/pallas_call | solution.py:498
  228.5 4.4 %all-to-all-start.5 = ((f32[16,144,128]{2,1,0:T(8,128)}), f32[16,144,128]{2,1,0:T(8,128)}, u32[]{:S(2)}, u32[]{:S(2)}) async-start(f32[16,144,128]{2,1,0:T(8,128)} %shard_map.107), calls=%async_computation.5 | async-start | bytes 2359296 | tf_op jit(solution)/shard_map/all_to_all | solution.py:530
  232.9 12.7 %collective-permute-done.7.far = f32[232,1024]{1,0:T(8,128)} collective-permute-done((f32[232,1024]{1,0:T(8,128)}, f32[232,1024]{1,0:T(8,128)}, u32[]{:S(2)}, u32[]{:S(2)}) %collective-permute-start.7) | collective-permute-done | bytes 950304 | tf_op jit(solution)/shard_map/ppermute | solution.py:618
  247.8 5.1 %collective-permute-start.8 = (f32[2304,128]{1,0:T(8,128)}, f32[2304,128]{1,0:T(8,128)}, u32[]{:S(2)}, u32[]{:S(2)}) collective-permute-start(f32[2304,128]{1,0:T(8,128)} %bitcast.10.mine), channel_id=1, source_target_pairs={{0,2},{2,0},{4,6},{6,4},{8,10},{10,8},{12,14},{14,12},{16,18},{18,... | collective-permute-start | bytes 3538952 | tf_op jit(solution)/shard_map/ppermute | solution.py:625
  252.9 2.8 %collective-permute-done.8.theirs = f32[2304,128]{1,0:T(8,128)} collective-permute-done((f32[2304,128]{1,0:T(8,128)}, f32[2304,128]{1,0:T(8,128)}, u32[]{:S(2)}, u32[]{:S(2)}) %collective-permute-start.8) | collective-permute-done | bytes 1179680 | tf_op jit(solution)/shard_map/ppermute | solution.py:625
  255.7 3.1 %shard_map.109 = f32[400,1345]{1,0:T(8,128)} custom-call(f32[2304,128]{1,0:T(8,128)} %bitcast.10.mine, f32[2304,128]{1,0:T(8,128)} %collective-permute-done.8.theirs), custom_call_target="tpu_custom_call" | custom-call | tf_op jit(solution)/shard_map/pallas_call | solution.py:498
  (34 shorter events, 24.5 us)
Async XLA Ops:
  1.4 7.5 %copy-start.3 = (s32[3,2,2560]{2,1,0:T(2,128)}, s32[3,2,2560]{2,1,0:T(2,128)S(1)}, u32[]{:S(2)}) copy-start(s32[3,2,2560]{2,1,0:T(2,128)S(1)} %pad_add_fusion.idx) | copy-start | bytes 184324
  1.4 7.5 %collective-permute-start = (s32[3,2,2560]{2,1,0:T(2,128)S(1)}, s32[3,2,2560]{2,1,0:T(2,128)S(1)}, u32[]{:S(2)}, u32[]{:S(2)}) collective-permute-start(s32[3,2,2560]{2,1,0:T(2,128)S(1)} %pad_add_fusion.idx), channel_id=1, source_target_pairs={{0,1},{1,0},{2,3},{3,2},{4,5},{5,4},{6,7},{7,6},{8,9},{9,8},{10,11... | collective-permute-start | bytes 184328 | tf_op jit(solution)/shard_map/ppermute | solution.py:535
  8.9 0.6 copy-start.5
  9.5 34.6 %all-to-all-start = ((bf16[64,112,128]{2,1,0:T(8,128)(2,1)}), bf16[64,112,128]{2,1,0:T(8,128)(2,1)}, u32[]{:S(2)}, u32[]{:S(2)}) async-start(bf16[64,112,128]{2,1,0:T(8,128)(2,1)} %shard_map.95), calls=%async_computation | async-start | bytes 3670016 | tf_op jit(solution)/shard_map/all_to_all | solution.py:530
  47.5 39.3 %all-to-all-start.1 = ((bf16[64,112,128]{2,1,0:T(8,128)(2,1)}), bf16[64,112,128]{2,1,0:T(8,128)(2,1)}, u32[]{:S(2)}, u32[]{:S(2)}) async-start(bf16[64,112,128]{2,1,0:T(8,128)(2,1)} %shard_map.97), calls=%async_computation.1 | async-start | bytes 3670016 | tf_op jit(solution)/shard_map/all_to_all | solution.py:530
  86.7 43.2 %collective-permute-start.1 = (f32[400,1024]{1,0:T(8,128)}, f32[400,1024]{1,0:T(8,128)}, u32[]{:S(2)}, u32[]{:S(2)}) collective-permute-start(f32[400,1024]{1,0:T(8,128)} %get-tuple-element.57), channel_id=1, source_target_pairs={{0,1},{1,0},{2,3},{3,2},{4,5},{5,4},{6,7},{7,6},{8,9},{9,8},{10,11... | collective-permute-start | bytes 4915208 | tf_op jit(solution)/shard_map/ppermute | solution.py:572
  118.6 36.8 %all-to-all-start.2 = ((f32[64,56,128]{2,1,0:T(8,128)}), f32[64,56,128]{2,1,0:T(8,128)}, u32[]{:S(2)}, u32[]{:S(2)}) async-start(f32[64,56,128]{2,1,0:T(8,128)} %get-tuple-element.61), calls=%async_computation.2 | async-start | bytes 3670016 | tf_op jit(solution)/shard_map/all_to_all | solution.py:530
  149.5 14.1 %collective-permute-start.2 = (f32[2304,128]{1,0:T(8,128)}, f32[2304,128]{1,0:T(8,128)}, u32[]{:S(2)}, u32[]{:S(2)}) collective-permute-start(f32[2304,128]{1,0:T(8,128)} %get-tuple-element.65), channel_id=1, source_target_pairs={{0,2},{2,0},{4,6},{6,4},{8,10},{10,8},{12,14},{14,12},{16,18},{18,... | collective-permute-start | bytes 3538952 | tf_op jit(solution)/shard_map/ppermute | solution.py:595
  158.1 31.1 %all-to-all-start.3 = ((f32[64,56,128]{2,1,0:T(8,128)}), f32[64,56,128]{2,1,0:T(8,128)}, u32[]{:S(2)}, u32[]{:S(2)}) async-start(f32[64,56,128]{2,1,0:T(8,128)} %shard_map.101), calls=%async_computation.3 | async-start | bytes 3670016 | tf_op jit(solution)/shard_map/all_to_all | solution.py:530
  192.6 18.2 %collective-permute-start.3 = (f32[168,1024]{1,0:T(8,128)}, f32[168,1024]{1,0:T(8,128)S(1)}, u32[]{:S(2)}, u32[]{:S(2)}) collective-permute-start(f32[168,1024]{1,0:T(8,128)} %get-tuple-element.72.first), channel_id=1, source_target_pairs={{0,1},{1,0},{2,3},{3,2},{4,5},{5,4},{6,7},{7,6},{8,9},{9,8},{10,11... | collective-permute-start | bytes 2064392 | tf_op jit(solution)/shard_map/ppermute | solution.py:608
  194.0 21.4 %all-to-all-start.4 = ((f32[16,144,128]{2,1,0:T(8,128)}), f32[16,144,128]{2,1,0:T(8,128)}, u32[]{:S(2)}, u32[]{:S(2)}) async-start(f32[16,144,128]{2,1,0:T(8,128)} %shard_map.103), calls=%async_computation.4 | async-start | bytes 2359296 | tf_op jit(solution)/shard_map/all_to_all | solution.py:530
  210.9 0.9 copy-start.4
  217.3 4.9 %collective-permute-start.6 = (f32[144,128]{1,0:T(8,128)}, f32[144,128]{1,0:T(8,128)S(1)}, u32[]{:S(2)}, u32[]{:S(2)}) collective-permute-start(f32[144,128]{1,0:T(8,128)} %shard_map.106.a), channel_id=1, source_target_pairs={{0,65},{1,64},{2,67},{3,66},{4,69},{5,68},{6,71},{7,70},{8,73},{9,... | collective-permute-start | bytes 221192 | tf_op jit(solution)/shard_map/ppermute | solution.py:616
  219.8 4.9 %collective-permute-start.5 = (f32[144,128]{1,0:T(8,128)}, f32[144,128]{1,0:T(8,128)S(1)}, u32[]{:S(2)}, u32[]{:S(2)}) collective-permute-start(f32[144,128]{1,0:T(8,128)} %shard_map.106.a), channel_id=1, source_target_pairs={{0,1},{1,0},{2,3},{3,2},{4,5},{5,4},{6,7},{7,6},{8,9},{9,8},{10,11... | collective-permute-start | bytes 221192 | tf_op jit(solution)/shard_map/ppermute | solution.py:615
  219.9 4.7 %collective-permute-start.4 = (f32[144,128]{1,0:T(8,128)}, f32[144,128]{1,0:T(8,128)S(1)}, u32[]{:S(2)}, u32[]{:S(2)}) collective-permute-start(f32[144,128]{1,0:T(8,128)} %shard_map.106.a), channel_id=1, source_target_pairs={{0,64},{2,66},{4,68},{6,70},{8,72},{10,74},{12,76},{14,78},{16,80}... | collective-permute-start | bytes 221192 | tf_op jit(solution)/shard_map/ppermute | solution.py:615
  222.2 4.2 %copy-start = (f32[144,128]{1,0:T(8,128)}, f32[144,128]{1,0:T(8,128)S(1)}, u32[]{:S(2)}) copy-start(f32[144,128]{1,0:T(8,128)S(1)} %collective-permute-done.6.d) | copy-start | bytes 221188
  224.7 1.7 copy-start.1
  224.7 1.7 copy-start.2
  224.7 20.9 %collective-permute-start.7 = (f32[232,1024]{1,0:T(8,128)}, f32[232,1024]{1,0:T(8,128)}, u32[]{:S(2)}, u32[]{:S(2)}) collective-permute-start(f32[232,1024]{1,0:T(8,128)} %get-tuple-element.79.second), channel_id=1, source_target_pairs={{0,1},{1,0},{2,3},{3,2},{4,5},{5,4},{6,7},{7,6},{8,9},{9,8},{10,11... | collective-permute-start | bytes 2850824 | tf_op jit(solution)/shard_map/ppermute | solution.py:618
  228.5 19.3 %all-to-all-start.5 = ((f32[16,144,128]{2,1,0:T(8,128)}), f32[16,144,128]{2,1,0:T(8,128)}, u32[]{:S(2)}, u32[]{:S(2)}) async-start(f32[16,144,128]{2,1,0:T(8,128)} %shard_map.107), calls=%async_computation.5 | async-start | bytes 2359296 | tf_op jit(solution)/shard_map/all_to_all | solution.py:530
  247.8 7.9 %collective-permute-start.8 = (f32[2304,128]{1,0:T(8,128)}, f32[2304,128]{1,0:T(8,128)}, u32[]{:S(2)}, u32[]{:S(2)}) collective-permute-start(f32[2304,128]{1,0:T(8,128)} %bitcast.10.mine), channel_id=1, source_target_pairs={{0,2},{2,0},{4,6},{6,4},{8,10},{10,8},{12,14},{14,12},{16,18},{18,... | collective-permute-start | bytes 3538952 | tf_op jit(solution)/shard_map/ppermute | solution.py:625

commit v5 on v4

--- a/solution.py
+++ b/solution.py
@@ -107,13 +107,12 @@
     rel_total[...] += nt(high, rel_marks[...]) + nt(low, rel_marks[...])
 
 
-def own_slot(position, slab, idx, own, rel_total, marks, rel_marks, neg, gathered):
-    lidx, ridx, relx, nidx = columns(position, 0, 0, (idx, None))
+def own_slot(position, slab, idx, own, marks, neg, gathered, keep_relation):
+    lidx, ridx, _, nidx = columns(position, 0, 0, (idx, None))
     edges, negatives = lidx.shape[1], nidx.shape[1]
     rows = slab.shape[1]
     mark(lidx, marks, slice(0, edges))
     mark(ridx, marks, slice(edges, 2 * edges))
-    mark(relx, rel_marks, slice(0, edges))
     h, rel, t = [x.astype(F32) for x in gathered()]
     query = product(h, rel)
     pos_grad = -sigmoid(-jnp.sum(query * t, axis=0, keepdims=True))
@@ -130,7 +129,7 @@
         own[:, at] += (
             nt(both_high, marks[at, :]) + nt(both_low, marks[at, :]) + nt(query_low, neg[at, :]) * counts[:, at]
         )
-    add_relations(conjugate(query_grad, h), rel_marks, rel_total)
+    keep_relation(*split(conjugate(query_grad, h)))
 
 
 def widen(relations, rel_wide):
@@ -202,7 +201,7 @@
 
 def own_kernel(
     counts, slab, idx, heads, rels, tails,
-    keep, give, rel_total, own, marks, rel_marks, neg, head, rel, tail, sems,
+    keep, give, rel_highs, rel_lows, own, marks, neg, head, rel, tail, rel_high, rel_low, sems, out_sems,
 ):
     side, _, near, _ = place(counts, idx.shape[0])
     last = near[0]
@@ -210,12 +209,14 @@
     def fetch(i):
         return streams((heads, rels, tails), (head, rel, tail), sems, i)
 
+    def away(i):
+        return streams((rel_highs, rel_lows), (rel_high, rel_low), out_sems, i, out=True)
+
     @pl.when(last >= 1)
     def _():
         begin(fetch(0))
 
     own[...] = jnp.zeros_like(own)
-    rel_total[...] = jnp.zeros_like(rel_total)
 
     def step(i):
         @pl.when(i + 1 < last)
@@ -226,9 +227,29 @@
             finish(fetch(i))
             return [buf[lax.rem(i, 2)] for buf in (head, rel, tail)]
 
-        own_slot(i, slab, idx, own, rel_total, marks, rel_marks, neg, gathered)
+        def keep_relation(high, low):
+            k = lax.rem(i, 2)
+
+            @pl.when(i >= 2)
+            def _():
+                finish(away(i - 2))
+
+            rel_high[k] = high
+            rel_low[k] = low
+            begin(away(i))
+
+        own_slot(i, slab, idx, own, marks, neg, gathered, keep_relation)
 
     repeat(0, last, step)
+
+    @pl.when(last >= 2)
+    def _():
+        finish(away(last - 2))
+
+    @pl.when(last >= 1)
+    def _():
+        finish(away(last - 1))
+
     middle = keep.shape[1]
 
     @pl.when(side == 0)
@@ -342,12 +363,33 @@
 
 
 def left_kernel(
-    counts, idx, theirs, weights, pos_grads, right, rels, tails, negs, heads, far_own, rel_in,
-    own, keep, give, rel_total, marks, rel_marks, rel, tail, neg, head, sems,
+    counts, idx, theirs, weights, pos_grads, right, rels, tails, negs, heads, far_own, rel_highs, rel_lows,
+    own, keep, give, rel_total, marks, rel_marks, rel, tail, neg, head, sems, rel_sems,
 ):
     side, core, near, _ = place(counts, idx.shape[0])
+
+    def fetch(i):
+        return streams((rel_highs, rel_lows), (rel, head), rel_sems, i)
+
+    @pl.when(near[0] >= 1)
+    def _():
+        begin(fetch(0))
+
     own[...] = jnp.zeros_like(own)
-    rel_total[...] = rel_in[...]
+    rel_total[...] = jnp.zeros_like(rel_total)
+
+    def step(i):
+        @pl.when(i + 1 < near[0])
+        def _():
+            begin(fetch(i + 1))
+
+        k = lax.rem(i, 2)
+        relx = columns(i, 0, 0, (idx, None))[2]
+        mark(relx, rel_marks, slice(0, relx.shape[1]))
+        finish(fetch(i))
+        rel_total[...] += nt(rel[k], rel_marks[...]) + nt(head[k], rel_marks[...])
+
+    repeat(0, near[0], step)
     left_steps(
         0, near[1], side, near[1], (idx, theirs), (weights, pos_grads, right, rels, tails, negs, heads),
         own, rel_total, marks, rel_marks, (rel, tail, neg, head), sems,
@@ -564,10 +606,10 @@
     held, heads = lax.optimization_barrier((held, heads))
     chosen = call(take_kernel, shape(held.shape, BF16), [SM, HB], [sem], matching, held)
     partner = exchange(chosen)
-    keep, give, rel_total = call(
-        own_kernel, (own_shape, own_shape, rel_shape), [SM] + [VM] * 2 + [HB] * 3,
-        [mem(width, rows, F32), two_marks, rel_marks, neg, two_wide, two_wide, two_wide, sems(3)],
-        group_counts, slab, packed, *own_rows, flops=32 * unit,
+    keep, give, rel_highs, rel_lows = call(
+        own_kernel, (own_shape, own_shape, near_gathered, near_gathered), [SM] + [VM] * 2 + [HB] * 3,
+        [mem(width, rows, F32), two_marks, neg] + [two_wide] * 5 + [sems(3), sems(2)],
+        group_counts, slab, packed, *own_rows, flops=32 * unit, out_specs=(VM, VM, HB, HB),
     )
     got = lax.ppermute(give, "edge", swap)
     other, pos_grads, right, tails, negs = call(
@@ -588,9 +630,9 @@
     rel_flat = shape((REL_RING * REL_WINDOW, LANES))
     saved = (weights, pos_grads, right, rel_rows, tails, negs)
     own, rel_keep, rel_give = call(
-        left_kernel, (own_shape, rel_flat, rel_flat), [SM] + [VM] * 5 + [HB] * 5 + [VM],
-        [mem(width, padded, F32), one_mark, rel_marks, two_wide, two_wide, two_neg, two_wide, sems(4)],
-        group_counts, *idx, *saved, heads, got, rel_total, flops=20 * unit,
+        left_kernel, (own_shape, rel_flat, rel_flat), [SM] + [VM] * 5 + [HB] * 7,
+        [mem(width, padded, F32), one_mark, rel_marks, two_wide, two_wide, two_neg, two_wide, sems(4), sems(2)],
+        group_counts, *idx, *saved, heads, got, rel_highs, rel_lows, flops=20 * unit,
     )
     rel_got = lax.ppermute(rel_give, "dom", cores)
     grad_chosen = call(put_kernel, shape(grad_held.shape), [SM, VM], [sem], matching, grad_held, out_specs=HB)

time: 260 us -> 259 us (level)
  Pallas kernels: 150 us -> 128 us
  waiting for transfers between devices: 48.3 us -> 59.7 us
  starting transfers between devices: 57.3 us -> 68 us
    pallas_call x15, Pallas kernels: 150 us -> 128 us  [call(): pl.pallas_call(kernel, out_shape=outs, in_specs=specs, out_specs=jax.tree...]
    all_to_all x6, waiting for transfers between devices: 16.2 us -> 27.1 us  [exchange(): lax.all_to_all(x, 'dom', split_axis=0, concat_axis=0, tiled=True, axis_in...]
    all_to_all x6, starting transfers between devices: 41.2 us -> 48.3 us  [exchange(): lax.all_to_all(x, 'dom', split_axis=0, concat_axis=0, tiled=True, axis_in...]
    ppermute x1, starting transfers between devices: 0.09 us -> 3.88 us  [body(): rel_got = lax.ppermute(rel_give, 'dom', cores)]
  transfers between devices with their start and end apart: 15 -> 15, of which waited for: 9 -> 10; matrix products, arithmetic and copies ran while one was open for 0% -> 0% of each run, Pallas kernels for 53% -> 45%
where the time goes in v5:
time: 259 us; the launch traced here: 258 us
  Pallas kernels  128 us (49%)
  starting transfers between devices  68 us (26%)
  waiting for transfers between devices  59.7 us (23%)
    pallas_call x15, Pallas kernels, call(): pl.pallas_call(kernel, out_shape=outs, in_specs=specs, out_specs=jax.tree...  128 us
    all_to_all x6, starting transfers between devices, exchange(): lax.all_to_all(x, 'dom', split_axis=0, concat_axis=0, tiled=True, axis_in...  48.3 us
    all_to_all x6, waiting for transfers between devices, exchange(): lax.all_to_all(x, 'dom', split_axis=0, concat_axis=0, tiled=True, axis_in...  27.1 us
    ppermute x1, waiting for transfers between devices, body(): far[1] = lax.ppermute(second, 'edge', swap)  12.7 us
    ppermute x1, waiting for transfers between devices, body(): far = [lax.ppermute(first, 'edge', swap), None]  12.7 us
  transfers between devices with their start and end apart: 15, of which 10 were waited for; matrix products, arithmetic and copies ran while one was open for 0% of the time, Pallas kernels for 45%

profile of v5, /device:TPU:1, one launch (start us, length us, event | category | flops | bytes accessed | tf_op | source)
XLA Modules:
  0.0 258.3 jit_solution(13245056026268852220)
XLA Ops:
  1.4 4.5 %collective-permute-start = (s32[3,2,2560]{2,1,0:T(2,128)S(1)}, s32[3,2,2560]{2,1,0:T(2,128)S(1)}, u32[]{:S(2)}, u32[]{:S(2)}) collective-permute-start(s32[3,2,2560]{2,1,0:T(2,128)S(1)} %pad_add_fusion.idx), channel_id=1, source_target_pairs={{0,1},{1,0},{2,3},{3,2},{4,5},{5,4},{6,7},{7,6},{8,9},{9,8},{10,11... | collective-permute-start | bytes 184328 | tf_op jit(solution)/shard_map/ppermute | solution.py:577
  5.9 3.0 %shard_map.95 = bf16[64,112,128]{2,1,0:T(8,128)(2,1)} custom-call(bf16[400,2048]{1,0:T(8,128)(2,1)} %bitcast.18), custom_call_target="tpu_custom_call" | custom-call | tf_op jit(solution)/shard_map/pallas_call | solution.py:540
  9.5 9.1 %all-to-all-start = ((bf16[64,112,128]{2,1,0:T(8,128)(2,1)}), bf16[64,112,128]{2,1,0:T(8,128)(2,1)}, u32[]{:S(2)}, u32[]{:S(2)}) async-start(bf16[64,112,128]{2,1,0:T(8,128)(2,1)} %shard_map.95), calls=%async_computation | async-start | bytes 3670016 | tf_op jit(solution)/shard_map/all_to_all | solution.py:572
  18.6 18.2 %shard_map.96 = (bf16[6,400,512]{2,1,0:T(8,128)(2,1)}, bf16[6,400,512]{2,1,0:T(8,128)(2,1)}, f32[6,1,2048]{2,1,0:T(1,128)}, bf16[3,400,512]{2,1,0:T(8,128)(2,1)}...) custom-call(s32[1,2]{1,0:T(1,128)} %counts.9, bf16[400,2048]{1,0:T(8,128)(2,1)} %bitcast.19, ...), custom_call_target="tpu_custom_call" | custom-call | flops 18454937600 | tf_op jit(solution)/shard_map/pallas_call | solution.py:540
  36.8 7.3 %all-to-all-done.held = bf16[64,112,128]{2,1,0:T(8,128)(2,1)} async-done(((bf16[64,112,128]{2,1,0:T(8,128)(2,1)}), bf16[64,112,128]{2,1,0:T(8,128)(2,1)}, u32[]{:S(2)}, u32[]{:S(2)}) %all-to-all-start) | async-done | bytes 1835040 | tf_op jit(solution)/shard_map/all_to_all | solution.py:572
  44.1 3.4 %shard_map.97 = bf16[64,112,128]{2,1,0:T(8,128)(2,1)} custom-call(s32[64]{0:T(128)} %matching.3, bf16[64,112,128]{2,1,0:T(8,128)(2,1)} %all-to-all-done.held), custom_call_target="tpu_custom_call" | custom-call | tf_op jit(solution)/shard_map/pallas_call | solution.py:540
  47.5 6.6 %all-to-all-start.1 = ((bf16[64,112,128]{2,1,0:T(8,128)(2,1)}), bf16[64,112,128]{2,1,0:T(8,128)(2,1)}, u32[]{:S(2)}, u32[]{:S(2)}) async-start(bf16[64,112,128]{2,1,0:T(8,128)(2,1)} %shard_map.97), calls=%async_computation.1 | async-start | bytes 3670016 | tf_op jit(solution)/shard_map/all_to_all | solution.py:572
  54.0 13.5 %shard_map.99 = (f32[400,1024]{1,0:T(8,128)}, f32[400,1024]{1,0:T(8,128)}, bf16[3,400,512]{2,1,0:T(8,128)(2,1)}, bf16[3,400,512]{2,1,0:T(8,128)(2,1)}) custom-call(s32[1,2]{1,0:T(1,128)} %counts.9, bf16[400,2048]{1,0:T(8,128)(2,1)} %bitcast.20, s32[3,2,2560]{2,1,0:T(2,128)} %copy-done.3, bf16[3,400,512]{2,1,0:T(8,128)(2,1)} %get-tuple-element.55.heads, ...), custom_call_target="tpu_custom_call" | custom-call | flops 26843545600 | tf_op jit(solution)/shard_map/pallas_call | solution.py:540
  67.7 11.9 %all-to-all-done.1.pieces = bf16[64,112,128]{2,1,0:T(8,128)(2,1)} async-done(((bf16[64,112,128]{2,1,0:T(8,128)(2,1)}), bf16[64,112,128]{2,1,0:T(8,128)(2,1)}, u32[]{:S(2)}, u32[]{:S(2)}) %all-to-all-start.1) | async-done | bytes 1835040 | tf_op jit(solution)/shard_map/all_to_all | solution.py:572
  79.6 31.5 %shard_map.98 = (f32[64,56,128]{2,1,0:T(8,128)}, f32[6,1,512]{2,1,0:T(1,128)}, bf16[400,2048]{1,0:T(8,128)(2,1)}, bf16[6,400,512]{2,1,0:T(8,128)(2,1)}, bf16[6,2048,512]{2,1,0:T(8,128)(2,1)}) custom-call(s32[1,2]{1,0:T(1,128)} %counts.9, bf16[64,112,128]{2,1,0:T(8,128)(2,1)} %all-to-all-done.1.pieces, s32[3,2,2560]{2,1,0:T(2,128)} %copy-done.3, ...), custom_call_target="tpu_custom_call" | custom-call | flops 25165824000 | tf_op jit(solution)/shard_map/pallas_call | solution.py:540
  111.0 15.4 %all-to-all-start.2 = ((f32[64,56,128]{2,1,0:T(8,128)}), f32[64,56,128]{2,1,0:T(8,128)}, u32[]{:S(2)}, u32[]{:S(2)}) async-start(f32[64,56,128]{2,1,0:T(8,128)} %get-tuple-element.63), calls=%async_computation.2 | async-start | bytes 3670016 | tf_op jit(solution)/shard_map/all_to_all | solution.py:572
  126.4 21.5 %shard_map.100 = (f32[400,1024]{1,0:T(8,128)}, f32[2304,128]{1,0:T(8,128)}, f32[2304,128]{1,0:T(8,128)}) custom-call(s32[1,2]{1,0:T(1,128)} %counts.9, s32[3,2,2560]{2,1,0:T(2,128)} %copy-done.3, s32[3,2,2560]{2,1,0:T(2,128)} %copy-done.5, f32[6,1,2048]{2,1,0:T(1,128)} %get-tuple-element.45.weights, f32[6,1,512]{2,1,0:T(1,128)} %get-tuple-element.51.pos_grads, ...), custom_call_target="tpu_custom_call" | custom-call | flops 16777216000 | tf_op jit(solution)/shard_map/pallas_call | solution.py:540
  147.9 3.9 %collective-permute-start.2 = (f32[2304,128]{1,0:T(8,128)}, f32[2304,128]{1,0:T(8,128)}, u32[]{:S(2)}, u32[]{:S(2)}) collective-permute-start(f32[2304,128]{1,0:T(8,128)} %get-tuple-element.67), channel_id=1, source_target_pairs={{0,2},{2,0},{4,6},{6,4},{8,10},{10,8},{12,14},{14,12},{16,18},{18,... | collective-permute-start | bytes 3538952 | tf_op jit(solution)/shard_map/ppermute | solution.py:637
  154.6 8.5 %all-to-all-start.3 = ((f32[64,56,128]{2,1,0:T(8,128)}), f32[64,56,128]{2,1,0:T(8,128)}, u32[]{:S(2)}, u32[]{:S(2)}) async-start(f32[64,56,128]{2,1,0:T(8,128)} %shard_map.101), calls=%async_computation.3 | async-start | bytes 3670016 | tf_op jit(solution)/shard_map/all_to_all | solution.py:572
  166.0 15.3 %shard_map.102.own = f32[400,1024]{1,0:T(8,128)} custom-call(s32[1,2]{1,0:T(1,128)} %counts.9, s32[3,2,2560]{2,1,0:T(2,128)} %copy-done.3, s32[3,2,2560]{2,1,0:T(2,128)} %copy-done.5, f32[6,1,2048]{2,1,0:T(1,128)} %get-tuple-element.45.weights, f32[6,1,512]{2,1,0:T(1,128)} %get-tuple-element.51.pos_grads, bf16[400,2048]{1,0:T(8,128)(2,1)} %get-tuple-element.52.right, ...), custom_call_target="tpu_custom_call" | custom-call | flops 12582912000 | tf_op jit(solution)/shard_map/pallas_call | solution.py:540
  181.3 7.4 %all-to-all-done.3.pieces = f32[64,56,128]{2,1,0:T(8,128)} async-done(((f32[64,56,128]{2,1,0:T(8,128)}), f32[64,56,128]{2,1,0:T(8,128)}, u32[]{:S(2)}, u32[]{:S(2)}) %all-to-all-start.3) | async-done | bytes 1835040 | tf_op jit(solution)/shard_map/all_to_all | solution.py:572
  188.7 3.4 %shard_map.104 = (f32[168,1024]{1,0:T(8,128)}, f32[232,1024]{1,0:T(8,128)}) custom-call(f32[400,1024]{1,0:T(8,128)} %shard_map.102.own, f32[64,56,128]{2,1,0:T(8,128)} %all-to-all-done.3.pieces), custom_call_target="tpu_custom_call" | custom-call | tf_op jit(solution)/shard_map/pallas_call | solution.py:540
  193.3 4.4 %all-to-all-start.4 = ((f32[16,144,128]{2,1,0:T(8,128)}), f32[16,144,128]{2,1,0:T(8,128)}, u32[]{:S(2)}, u32[]{:S(2)}) async-start(f32[16,144,128]{2,1,0:T(8,128)} %shard_map.103), calls=%async_computation.4 | async-start | bytes 2359296 | tf_op jit(solution)/shard_map/all_to_all | solution.py:572
  197.7 12.7 %collective-permute-done.3.far = f32[168,1024]{1,0:T(8,128)S(1)} collective-permute-done((f32[168,1024]{1,0:T(8,128)}, f32[168,1024]{1,0:T(8,128)S(1)}, u32[]{:S(2)}, u32[]{:S(2)}) %collective-permute-start.3) | collective-permute-done | bytes 688160 | tf_op jit(solution)/shard_map/ppermute | solution.py:650
  211.2 3.0 %shard_map.105.begun = f32[400,2048]{1,0:T(8,128)} custom-call(f32[168,1024]{1,0:T(8,128)} %get-tuple-element.74.first, f32[232,1024]{1,0:T(8,128)} %get-tuple-element.81.second, f32[168,1024]{1,0:T(8,128)} %copy-done.4), custom_call_target="tpu_custom_call" | custom-call | flops 50331648000 | tf_op jit(solution)/shard_map/pallas_call | solution.py:540
  228.0 4.4 %all-to-all-start.5 = ((f32[16,144,128]{2,1,0:T(8,128)}), f32[16,144,128]{2,1,0:T(8,128)}, u32[]{:S(2)}, u32[]{:S(2)}) async-start(f32[16,144,128]{2,1,0:T(8,128)} %shard_map.107), calls=%async_computation.5 | async-start | bytes 2359296 | tf_op jit(solution)/shard_map/all_to_all | solution.py:572
  232.4 12.7 %collective-permute-done.7.far = f32[232,1024]{1,0:T(8,128)} collective-permute-done((f32[232,1024]{1,0:T(8,128)}, f32[232,1024]{1,0:T(8,128)}, u32[]{:S(2)}, u32[]{:S(2)}) %collective-permute-start.7) | collective-permute-done | bytes 950304 | tf_op jit(solution)/shard_map/ppermute | solution.py:660
  247.3 5.1 %collective-permute-start.8 = (f32[2304,128]{1,0:T(8,128)}, f32[2304,128]{1,0:T(8,128)}, u32[]{:S(2)}, u32[]{:S(2)}) collective-permute-start(f32[2304,128]{1,0:T(8,128)} %bitcast.10.mine), channel_id=1, source_target_pairs={{0,2},{2,0},{4,6},{6,4},{8,10},{10,8},{12,14},{14,12},{16,18},{18,... | collective-permute-start | bytes 3538952 | tf_op jit(solution)/shard_map/ppermute | solution.py:667
  255.2 3.1 %shard_map.109 = f32[400,1345]{1,0:T(8,128)} custom-call(f32[2304,128]{1,0:T(8,128)} %bitcast.10.mine, f32[2304,128]{1,0:T(8,128)} %collective-permute-done.8.theirs), custom_call_target="tpu_custom_call" | custom-call | tf_op jit(solution)/shard_map/pallas_call | solution.py:540
  (34 shorter events, 27.8 us)
Async XLA Ops:
  1.4 7.5 %copy-start.3 = (s32[3,2,2560]{2,1,0:T(2,128)}, s32[3,2,2560]{2,1,0:T(2,128)S(1)}, u32[]{:S(2)}) copy-start(s32[3,2,2560]{2,1,0:T(2,128)S(1)} %pad_add_fusion.idx) | copy-start | bytes 184324
  1.4 7.5 %collective-permute-start = (s32[3,2,2560]{2,1,0:T(2,128)S(1)}, s32[3,2,2560]{2,1,0:T(2,128)S(1)}, u32[]{:S(2)}, u32[]{:S(2)}) collective-permute-start(s32[3,2,2560]{2,1,0:T(2,128)S(1)} %pad_add_fusion.idx), channel_id=1, source_target_pairs={{0,1},{1,0},{2,3},{3,2},{4,5},{5,4},{6,7},{7,6},{8,9},{9,8},{10,11... | collective-permute-start | bytes 184328 | tf_op jit(solution)/shard_map/ppermute | solution.py:577
  8.9 0.6 copy-start.5
  9.5 34.6 %all-to-all-start = ((bf16[64,112,128]{2,1,0:T(8,128)(2,1)}), bf16[64,112,128]{2,1,0:T(8,128)(2,1)}, u32[]{:S(2)}, u32[]{:S(2)}) async-start(bf16[64,112,128]{2,1,0:T(8,128)(2,1)} %shard_map.95), calls=%async_computation | async-start | bytes 3670016 | tf_op jit(solution)/shard_map/all_to_all | solution.py:572
  47.5 32.1 %all-to-all-start.1 = ((bf16[64,112,128]{2,1,0:T(8,128)(2,1)}), bf16[64,112,128]{2,1,0:T(8,128)(2,1)}, u32[]{:S(2)}, u32[]{:S(2)}) async-start(bf16[64,112,128]{2,1,0:T(8,128)(2,1)} %shard_map.97), calls=%async_computation.1 | async-start | bytes 3670016 | tf_op jit(solution)/shard_map/all_to_all | solution.py:572
  67.6 58.9 %collective-permute-start.1 = (f32[400,1024]{1,0:T(8,128)}, f32[400,1024]{1,0:T(8,128)}, u32[]{:S(2)}, u32[]{:S(2)}) collective-permute-start(f32[400,1024]{1,0:T(8,128)} %get-tuple-element.58), channel_id=1, source_target_pairs={{0,1},{1,0},{2,3},{3,2},{4,5},{5,4},{6,7},{7,6},{8,9},{9,8},{10,11... | collective-permute-start | bytes 4915208 | tf_op jit(solution)/shard_map/ppermute | solution.py:614
  111.0 40.9 %all-to-all-start.2 = ((f32[64,56,128]{2,1,0:T(8,128)}), f32[64,56,128]{2,1,0:T(8,128)}, u32[]{:S(2)}, u32[]{:S(2)}) async-start(f32[64,56,128]{2,1,0:T(8,128)} %get-tuple-element.63), calls=%async_computation.2 | async-start | bytes 3670016 | tf_op jit(solution)/shard_map/all_to_all | solution.py:572
  147.9 15.3 %collective-permute-start.2 = (f32[2304,128]{1,0:T(8,128)}, f32[2304,128]{1,0:T(8,128)}, u32[]{:S(2)}, u32[]{:S(2)}) collective-permute-start(f32[2304,128]{1,0:T(8,128)} %get-tuple-element.67), channel_id=1, source_target_pairs={{0,2},{2,0},{4,6},{6,4},{8,10},{10,8},{12,14},{14,12},{16,18},{18,... | collective-permute-start | bytes 3538952 | tf_op jit(solution)/shard_map/ppermute | solution.py:637
  154.6 34.1 %all-to-all-start.3 = ((f32[64,56,128]{2,1,0:T(8,128)}), f32[64,56,128]{2,1,0:T(8,128)}, u32[]{:S(2)}, u32[]{:S(2)}) async-start(f32[64,56,128]{2,1,0:T(8,128)} %shard_map.101), calls=%async_computation.3 | async-start | bytes 3670016 | tf_op jit(solution)/shard_map/all_to_all | solution.py:572
  192.1 18.2 %collective-permute-start.3 = (f32[168,1024]{1,0:T(8,128)}, f32[168,1024]{1,0:T(8,128)S(1)}, u32[]{:S(2)}, u32[]{:S(2)}) collective-permute-start(f32[168,1024]{1,0:T(8,128)} %get-tuple-element.74.first), channel_id=1, source_target_pairs={{0,1},{1,0},{2,3},{3,2},{4,5},{5,4},{6,7},{7,6},{8,9},{9,8},{10,11... | collective-permute-start | bytes 2064392 | tf_op jit(solution)/shard_map/ppermute | solution.py:650
  193.3 21.4 %all-to-all-start.4 = ((f32[16,144,128]{2,1,0:T(8,128)}), f32[16,144,128]{2,1,0:T(8,128)}, u32[]{:S(2)}, u32[]{:S(2)}) async-start(f32[16,144,128]{2,1,0:T(8,128)} %shard_map.103), calls=%async_computation.4 | async-start | bytes 2359296 | tf_op jit(solution)/shard_map/all_to_all | solution.py:572
  210.4 0.8 copy-start.4
  216.6 5.1 %collective-permute-start.6 = (f32[144,128]{1,0:T(8,128)}, f32[144,128]{1,0:T(8,128)S(1)}, u32[]{:S(2)}, u32[]{:S(2)}) collective-permute-start(f32[144,128]{1,0:T(8,128)} %shard_map.106.a), channel_id=1, source_target_pairs={{0,65},{1,64},{2,67},{3,66},{4,69},{5,68},{6,71},{7,70},{8,73},{9,... | collective-permute-start | bytes 221192 | tf_op jit(solution)/shard_map/ppermute | solution.py:658
  219.2 4.9 %collective-permute-start.5 = (f32[144,128]{1,0:T(8,128)}, f32[144,128]{1,0:T(8,128)S(1)}, u32[]{:S(2)}, u32[]{:S(2)}) collective-permute-start(f32[144,128]{1,0:T(8,128)} %shard_map.106.a), channel_id=1, source_target_pairs={{0,1},{1,0},{2,3},{3,2},{4,5},{5,4},{6,7},{7,6},{8,9},{9,8},{10,11... | collective-permute-start | bytes 221192 | tf_op jit(solution)/shard_map/ppermute | solution.py:657
  219.4 4.8 %collective-permute-start.4 = (f32[144,128]{1,0:T(8,128)}, f32[144,128]{1,0:T(8,128)S(1)}, u32[]{:S(2)}, u32[]{:S(2)}) collective-permute-start(f32[144,128]{1,0:T(8,128)} %shard_map.106.a), channel_id=1, source_target_pairs={{0,64},{2,66},{4,68},{6,70},{8,72},{10,74},{12,76},{14,78},{16,80}... | collective-permute-start | bytes 221192 | tf_op jit(solution)/shard_map/ppermute | solution.py:657
  221.7 4.2 %copy-start = (f32[144,128]{1,0:T(8,128)}, f32[144,128]{1,0:T(8,128)S(1)}, u32[]{:S(2)}) copy-start(f32[144,128]{1,0:T(8,128)S(1)} %collective-permute-done.6.d) | copy-start | bytes 221188
  224.2 1.7 copy-start.1
  224.2 1.7 copy-start.2
  224.2 20.9 %collective-permute-start.7 = (f32[232,1024]{1,0:T(8,128)}, f32[232,1024]{1,0:T(8,128)}, u32[]{:S(2)}, u32[]{:S(2)}) collective-permute-start(f32[232,1024]{1,0:T(8,128)} %get-tuple-element.81.second), channel_id=1, source_target_pairs={{0,1},{1,0},{2,3},{3,2},{4,5},{5,4},{6,7},{7,6},{8,9},{9,8},{10,11... | collective-permute-start | bytes 2850824 | tf_op jit(solution)/shard_map/ppermute | solution.py:660
  228.0 19.3 %all-to-all-start.5 = ((f32[16,144,128]{2,1,0:T(8,128)}), f32[16,144,128]{2,1,0:T(8,128)}, u32[]{:S(2)}, u32[]{:S(2)}) async-start(f32[16,144,128]{2,1,0:T(8,128)} %shard_map.107), calls=%async_computation.5 | async-start | bytes 2359296 | tf_op jit(solution)/shard_map/all_to_all | solution.py:572
  247.3 7.9 %collective-permute-start.8 = (f32[2304,128]{1,0:T(8,128)}, f32[2304,128]{1,0:T(8,128)}, u32[]{:S(2)}, u32[]{:S(2)}) collective-permute-start(f32[2304,128]{1,0:T(8,128)} %bitcast.10.mine), channel_id=1, source_target_pairs={{0,2},{2,0},{4,6},{6,4},{8,10},{10,8},{12,14},{14,12},{16,18},{18,... | collective-permute-start | bytes 3538952 | tf_op jit(solution)/shard_map/ppermute | solution.py:667
